TPU v7x, 32 devices: a whole 2x2x4 slice. The times are simulated.
32 devices in a mesh: seq: 16 (over z, y, core), col: 2 (over x).
Axes of the slice: x: 2, y: 2, z: 4, core: 2. Of those that a mesh axis runs over, the one named last changes fastest.
Arguments:
- memory: bfloat16 [2048, 4096], P('col', 'seq'), may hold values from -8 to 8
- query: bfloat16 [4096, 2048], P('seq', 'col'), may hold values from -400 to 400
- out_grad: bfloat16 [4096, 2048], P('seq', 'col'), may hold values from -96 to 96
- w_key: bfloat16 [4096, 2048], P(None, 'col'), may hold values from -0.09375 to 0.09375
- w_value: bfloat16 [4096, 2048], P(None, 'col'), may hold values from -0.09375 to 0.09375
Outputs:
- d_query: bfloat16 [4096, 2048], P('seq', 'col')
- d_memory: bfloat16 [2048, 4096], P('col', 'seq')
All inputs are finite; a program needn't handle non-finite values.
Results may differ from a plain program's by a relative error of at most 0.02.
The roundings to bfloat16 on the way count: a program that leaves them out, or rounds other values in their place, can miss the bound.
Values may be sent and summed in bfloat16 or wider, within the bound.
No kernel may reach another device: no remote copies, remote signals or barrier semaphores. Data moves between devices by JAX's collectives and lax.ppermute only.
A program may use at most 128 MiB of HBM per device.

v0:
```python
import functools
import math

import jax
import jax.numpy as jnp
from jax import lax
from jax.experimental import pallas as pl
from jax.experimental.pallas import tpu as pltpu
from jax.sharding import PartitionSpec as P

HD = 64
F32 = jnp.float32
BF16 = jnp.bfloat16
VMEM = pl.BlockSpec(memory_space=pltpu.VMEM)
SMEM = pl.BlockSpec(memory_space=pltpu.SMEM)
MIB = 1024 * 1024


def dot(a, b, over_a, over_b):
    return lax.dot_general(
        a, b, (((over_a,), (over_b,)), ((), ())), preferred_element_type=F32
    )


def whole(kernel, out, *args, after=(), scratch=(), limit=16, flops=0):
    n = len(args)
    moved = sum(x.size * x.dtype.itemsize for x in args)
    return pl.pallas_call(
        lambda *refs: kernel(*refs[:n], *refs[n + len(after) :]),
        in_specs=[SMEM if x.dtype == jnp.int32 else VMEM for x in args]
        + [pl.BlockSpec(memory_space=pl.ANY)] * len(after),
        out_specs=[VMEM] * len(out),
        out_shape=out,
        scratch_shapes=scratch,
        compiler_params=pltpu.CompilerParams(vmem_limit_bytes=limit * MIB),
        cost_estimate=pl.CostEstimate(flops=flops, bytes_accessed=moved, transcendentals=0),
    )(*args, *after)


def head_of(x, h):
    return x[:, h * HD : (h + 1) * HD]


def pair_heads(query, out_grad):
    tgt, width = query.shape

    def kernel(q_ref, g_ref, out_ref):
        for h in range(width // HD):
            cols = pl.ds(h * HD, HD)
            out_ref[h] = jnp.concatenate([q_ref[:, cols], g_ref[:, cols]], axis=1)

    out = [jax.ShapeDtypeStruct((width // HD, tgt, 2 * HD), BF16)]
    return whole(kernel, out, query, out_grad)[0]


def pair_targets(query, out_grad, me, spans):
    tgt, width = query.shape
    place = [(i, at) for i, span in enumerate(spans) for at in range(len(span))]
    out = [
        jax.ShapeDtypeStruct((len(span), 2, tgt, 2 * HD), BF16) for span in spans for _ in range(2)
    ]

    def kernel(me_ref, q_ref, g_ref, *rest):
        out_refs, paired = rest[:-1], rest[-1]
        for h in range(width // HD):
            cols = pl.ds(h * HD, HD)
            paired[h] = jnp.concatenate([q_ref[:, cols], g_ref[:, cols]], axis=1)
        for i, at in place:
            for bits in range(4):
                head = (4 * spans[i][at] + bits) ^ me_ref[0]
                out_refs[2 * i + bits // 2][at, bits % 2] = paired[head]

    scratch = [pltpu.VMEM((width // HD, tgt, 2 * HD), BF16)]
    return whole(kernel, out, me, query, out_grad, scratch=scratch)


def cross(kept, came, after=()):
    n = kept.shape[0]

    def kernel(kept_ref, came_ref, first_ref, *second_refs):
        for i, ref in enumerate((kept_ref, came_ref)):
            first_ref[:, i] = ref[:, 0]
            for d, second_ref in enumerate(second_refs):
                second_ref[i] = ref[d, 1]

    out = [jax.ShapeDtypeStruct(kept.shape, kept.dtype)] + [jax.ShapeDtypeStruct(kept.shape[1:], kept.dtype)] * n
    first, *second = whole(kernel, out, kept, came, after=after)
    return first, second


def join(kept, came, after=()):
    def kernel(kept_ref, *refs):
        for d in range(len(came)):
            out_ref = refs[len(came) + d]
            out_ref[0] = kept_ref[d]
            out_ref[1] = refs[d][...]

    out = [jax.ShapeDtypeStruct((2, *kept.shape[1:]), kept.dtype)] * kept.shape[0]
    return whole(kernel, out, kept, *came, after=after)


def part_ways(pieces, after=()):
    def kernel(*refs):
        kept_ref, left_ref = refs[-2:]
        for d, ref in enumerate(refs[:-2]):
            kept_ref[d] = ref[0]
            left_ref[d] = ref[1]

    out = [jax.ShapeDtypeStruct((len(pieces), *pieces[0].shape[1:]), pieces[0].dtype)] * 2
    return whole(kernel, out, *pieces, after=after)


def concat(pieces, after=()):
    rows = [x.shape[0] for x in pieces]

    def kernel(*refs):
        at = 0
        for ref, n in zip(refs[:-1], rows):
            refs[-1][at : at + n] = ref[...]
            at += n

    out = [jax.ShapeDtypeStruct((sum(rows), *pieces[0].shape[1:]), pieces[0].dtype)]
    return whole(kernel, out, *pieces, after=after)[0]


def project(mem, w_key, w_value, before=None, after=()):
    blocks, rows, depth = mem.shape
    depth *= blocks
    width = w_key.shape[1]
    heads = width // HD
    tile = math.gcd(width, 256)
    ahead = 0 if before is None else before.shape[1]

    def kernel(m_ref, k_ref, v_ref, *refs):
        out_ref = refs[-1]
        if ahead:
            out_ref[:, :ahead, :] = refs[0][...]
        m = jnp.concatenate([m_ref[b] for b in range(blocks)], axis=1)
        for at in range(0, width, tile):
            key = dot(m, k_ref[:, at : at + tile], 1, 0).astype(BF16)
            value = dot(m, v_ref[:, at : at + tile], 1, 0).astype(BF16)
            for h in range(tile // HD):
                out_ref[at // HD + h, ahead:, :] = jnp.concatenate(
                    [head_of(key, h), head_of(value, h)], axis=1
                )

    out = [jax.ShapeDtypeStruct((heads, ahead + rows, 2 * HD), BF16)]
    args = (mem, w_key, w_value) + (() if before is None else (before,))
    return whole(kernel, out, *args, after=after, flops=4 * rows * depth * width)[0]


def memory_grad(dkv, at, rows, w_key, w_value, blocks, dtype, span=(0, 1), after=()):
    heads = dkv.shape[0]
    depth, width = w_key.shape
    each = depth // blocks
    tile = max(each, math.gcd(depth, 512))
    low, high = (int(depth * x) // tile * tile for x in span)

    def kernel(d_ref, k_ref, v_ref, out_ref):
        d = [d_ref[h, at : at + rows, :] for h in range(heads)]
        dk = jnp.concatenate([x[:, :HD] for x in d], axis=1)
        dv = jnp.concatenate([x[:, HD:] for x in d], axis=1)
        for start in range(low, high, tile):
            here = pl.ds(start, tile)
            part = dot(k_ref[here, :], dk, 1, 1) + dot(v_ref[here, :], dv, 1, 1)
            part = part.T.astype(dtype)
            for b in range(tile // each):
                out_ref[(start - low) // each + b] = part[:, b * each : (b + 1) * each]

    out = [jax.ShapeDtypeStruct(((high - low) // each, rows, each), dtype)]
    flops = 4 * rows * (high - low) * width
    return whole(kernel, out, dkv, w_key, w_value, after=after, flops=flops)[0]


def project_and_fetch(mem, w_key, w_value):
    blocks, rows, each = mem.shape
    depth, width = w_key.shape
    heads = width // HD
    steps = math.gcd(blocks, 8)
    tall, per = depth // steps, blocks // steps

    def kernel(m_ref, k_hbm, v_hbm, out_ref, k_ref, v_ref, key_ref, value_ref, sem):
        copies = []
        for i in range(steps):
            here = pl.ds(i * tall, tall)
            copies.append(
                [
                    pltpu.make_async_copy(k_hbm.at[here], k_ref.at[here], sem.at[0, i]),
                    pltpu.make_async_copy(v_hbm.at[here], v_ref.at[here], sem.at[1, i]),
                ]
            )
        for pair in copies:
            for copy in pair:
                copy.start()
        for i, pair in enumerate(copies):
            here = pl.ds(i * tall, tall)
            m = jnp.concatenate([m_ref[b] for b in range(i * per, (i + 1) * per)], axis=1)
            for copy, ref, sum_ref in zip(pair, (k_ref, v_ref), (key_ref, value_ref)):
                copy.wait()
                part = dot(m, ref[here, :], 1, 0)
                sum_ref[...] = part if i == 0 else sum_ref[...] + part
        key, value = key_ref[...].astype(BF16), value_ref[...].astype(BF16)
        for h in range(heads):
            out_ref[h] = jnp.concatenate([head_of(key, h), head_of(value, h)], axis=1)

    anywhere = pl.BlockSpec(memory_space=pl.ANY)
    return pl.pallas_call(
        kernel,
        in_specs=[VMEM, anywhere, anywhere],
        out_specs=[VMEM] * 3,
        out_shape=[
            jax.ShapeDtypeStruct((heads, rows, 2 * HD), BF16),
            pltpu.VMEM(w_key.shape, BF16),
            pltpu.VMEM(w_value.shape, BF16),
        ],
        scratch_shapes=[
            pltpu.VMEM((rows, width), F32),
            pltpu.VMEM((rows, width), F32),
            pltpu.SemaphoreType.DMA((2, steps)),
        ],
        compiler_params=pltpu.CompilerParams(vmem_limit_bytes=12 * MIB),
        cost_estimate=pl.CostEstimate(
            flops=4 * rows * depth * width, bytes_accessed=4 * depth * width, transcendentals=0
        ),
    )(mem, *[pltpu.with_memory_space_constraint(w, pltpu.MemorySpace.HBM) for w in (w_key, w_value)])


def add_up(parts, others, after=()):
    def kernel(*refs):
        out_ref, at = refs[-1], 0
        for ref in refs[: len(parts)]:
            here = pl.ds(at, ref.shape[0])
            total = ref[...]
            for other in refs[len(parts) : -1]:
                total = total + other[here].astype(F32)
            out_ref[here] = total.astype(BF16)
            at += ref.shape[0]

    out = [jax.ShapeDtypeStruct((sum(x.shape[0] for x in parts), *parts[0].shape[1:]), BF16)]
    return whole(kernel, out, *parts, *others, after=after)[0]


def unpack_query_grad(kept, came, me):
    far, _, half, wide = kept.shape
    heads = 4 * far

    def kernel(me_ref, kept_ref, came_ref, out_ref, by_head):
        for d in range(far):
            for bits in range(4):
                ref = came_ref if bits // 2 else kept_ref
                by_head[(4 * d + bits) ^ me_ref[0]] = ref[d, bits % 2]
        for side in range(2):
            rows = [by_head[h][:, side * HD : (side + 1) * HD] for h in range(heads)]
            out_ref[pl.ds(side * half, half), :] = jnp.concatenate(rows, axis=1)

    out = [jax.ShapeDtypeStruct((2 * half, heads * HD), BF16)]
    return whole(kernel, out, me, kept, came, scratch=[pltpu.VMEM((heads, half, wide), BF16)])[0]


def fold_rows(x, combine):
    return combine(x.reshape(x.shape[0] // 8, 8, x.shape[1]), axis=0)


def attention_kernel(tile, chunk, rows, first, last, qg_ref, kv_ref, *refs):
    step = pl.program_id(1)
    begin = (pl.program_id(0) == 0) & (step == 0)
    end = (pl.program_id(0) == pl.num_programs(0) - 1) & (step == pl.num_programs(1) - 1)
    if not first:
        before_ref, *refs = refs
    if last:
        wk_ref, wv_ref, dq_ref, dkv_ref, wk_out, wv_out, sem, *refs = refs
    else:
        dq_ref, dkv_ref, *refs = refs
    s_ref, e_ref, p_ref, acc_ref, kt_ref = refs

    fetches = []
    if last:
        fetches.append(pltpu.make_async_copy(wk_ref, wk_out, sem.at[0]))
        fetches.append(pltpu.make_async_copy(wv_ref, wv_out, sem.at[1]))

    @pl.when(begin)
    def _():
        for fetch in fetches:
            fetch.start()

    src, tgt = kv_ref.shape[0], qg_ref.shape[0]
    factor = 1.0 / math.sqrt(HD)
    slope = factor * math.log2(math.e)

    @pl.when(step == 0)
    def _():
        acc_ref[...] = jnp.zeros_like(acc_ref) if first else before_ref[...]
        kt_ref[...] = kv_ref[...].T[:HD]

    chunks = [pl.ds(at, chunk) for at in range(0, src, chunk)]
    tiles = tgt // tile

    def load(t):
        qg = qg_ref[pl.ds(pl.multiple_of(t * tile, tile), tile), :]
        in_query = lax.broadcasted_iota(jnp.int32, qg.shape, 1) < HD
        zero = jnp.zeros_like(qg)
        return jnp.where(in_query, qg, zero), jnp.where(in_query, zero, qg)

    def advance(t, carry, scores=True, weigh=True, grads=True):
        last_top, inverse, delta = carry
        top = total = inner = dq = None
        if scores:
            q_only, _ = load(t)
        if weigh:
            _, g_last = load(t - 1)
        if grads:
            q, g = load(t - 2)
            both = jnp.concatenate([g, q], axis=0)
        for here in chunks:
            if grads:
                weights = e_ref[here, :] * inverse
                grad = (weights * (p_ref[here, :] - delta)).astype(BF16)
                pair = jnp.concatenate([weights.astype(BF16), grad], axis=1)
                acc_ref[here, :] += dot(pair, both, 1, 0)
                part = dot(kt_ref[:, here], grad, 1, 0)
                dq = part if dq is None else dq + part
            if weigh:
                expo = jnp.exp2((s_ref[here, :] - last_top) * slope)
                p = dot(kv_ref[here, :], g_last, 1, 1)
                e_ref[here, :] = expo
                p_ref[here, :] = p
                sums = fold_rows(expo, jnp.sum), fold_rows(expo * p, jnp.sum)
                total, inner = sums if total is None else (total + sums[0], inner + sums[1])
            if scores:
                s = dot(kv_ref[here, :], q_only, 1, 1)
                s_ref[here, :] = s
                s = fold_rows(s, jnp.max)
                top = s if top is None else jnp.maximum(top, s)
        if grads:
            dq = (dq * factor).T
            half = rows // 2
            for at in range(0, tile, rows):
                to = pl.multiple_of((t - 2) * (tile // 2) + at // 2, half)
                dq_ref[pl.ds(to, half), :] = jnp.concatenate(
                    [dq[at : at + half], dq[at + half : at + rows]], axis=1
                ).astype(BF16)
        if weigh:
            inverse = 1.0 / jnp.sum(total, axis=0, keepdims=True)
            delta = jnp.sum(inner, axis=0, keepdims=True) * inverse
        if scores:
            last_top = jnp.max(top, axis=0, keepdims=True)
        return last_top, inverse, delta

    nothing = jnp.zeros((1, tile), F32)
    carry = advance(0, (nothing,) * 3, weigh=False, grads=False)
    if tiles > 1:
        carry = advance(1, carry, grads=False)
        carry = lax.fori_loop(2, tiles, advance, carry)
    carry = advance(tiles, carry, scores=False, grads=tiles > 1)
    advance(tiles + 1, carry, scores=False, weigh=False)

    @pl.when(step == pl.num_programs(1) - 1)
    def _():
        acc = acc_ref[...]
        if last:
            in_key = lax.broadcasted_iota(jnp.int32, acc.shape, 1) < HD
            acc = jnp.where(in_key, acc * factor, acc)
        dkv_ref[...] = acc.astype(dkv_ref.dtype)

    @pl.when(end)
    def _():
        for fetch in fetches:
            fetch.wait()


def attention(qg, kv, rows, before=None, weights=(), block=2048, tile=256, chunk=512):
    heads, tgt, wide = qg.shape
    src = kv.shape[1]
    first, last = before is None, bool(weights)
    work = heads * tgt * src
    tile = max(math.gcd(tgt, tile), rows)
    block = max(math.gcd(tgt, block), tile)
    weights = [pltpu.with_memory_space_constraint(w, pltpu.MemorySpace.HBM) for w in weights]
    every = pl.BlockSpec((None, src, wide), lambda h, i: (h, 0, 0))
    anywhere = pl.BlockSpec(memory_space=pl.ANY)
    return pl.pallas_call(
        functools.partial(attention_kernel, tile, math.gcd(src, chunk), rows, first, last),
        grid=(heads, tgt // block),
        in_specs=[pl.BlockSpec((None, block, wide), lambda h, i: (h, i, 0)), every]
        + [every] * (not first)
        + [anywhere] * len(weights),
        out_specs=[pl.BlockSpec((None, block // 2, wide), lambda h, i: (h, i, 0)), every]
        + [anywhere] * len(weights),
        out_shape=[
            jax.ShapeDtypeStruct((heads, tgt // 2, wide), BF16),
            jax.ShapeDtypeStruct((heads, src, wide), BF16 if last else F32),
        ]
        + [pltpu.VMEM(w.shape, w.dtype) for w in weights],
        scratch_shapes=[pltpu.SemaphoreType.DMA((2,))] * last
        + [
            pltpu.VMEM((src, tile), F32),
            pltpu.VMEM((src, tile), F32),
            pltpu.VMEM((src, tile), F32),
            pltpu.VMEM((src, wide), F32),
            pltpu.VMEM((HD, src), BF16),
        ],
        compiler_params=pltpu.CompilerParams(vmem_limit_bytes=32 * MIB),
        cost_estimate=pl.CostEstimate(
            flops=5 * 8 * work * HD, bytes_accessed=8 * heads * (tgt + src) * wide, transcendentals=work
        ),
    )(qg, kv, *(() if first else (before,)), *weights)


def local(seq, col, memory, query, out_grad, w_key, w_value):
    tgt, width = query.shape
    heads = width // HD
    groups = math.gcd(heads, seq)
    ranges = seq // groups
    each = heads // groups
    same_range = [[r * groups + g for g in range(groups)] for r in range(ranges)]
    same_heads = [[r * groups + g for r in range(ranges)] for g in range(groups)]
    pairwise = ranges == 1 and each == 1 and groups >= 16 and groups & (groups - 1) == 0
    me = lax.axis_index("seq").astype(jnp.int32) if pairwise else jnp.int32(0)
    me = me.reshape(1)
    far = groups // 4

    def deal(x):
        return lax.all_to_all(x, "seq", 0, 0, tiled=True, axis_index_groups=same_range)

    def swap(x, bits):
        return lax.ppermute(x, "seq", [(i, i ^ bits) for i in range(seq)])

    def gather_far(x, d):
        return swap(x, 4 * d) if d else x

    def by_head(x, many):
        x = x.reshape(many, each, *x.shape[1:]).swapaxes(0, 1)
        return x.reshape(each, many * x.shape[2], x.shape[3])

    def by_owner(x, many):
        x = x.reshape(each, many, x.shape[1] // many, x.shape[2]).swapaxes(0, 1)
        return x.reshape(many * each, *x.shape[2:])

    def shift(x, by):
        return lax.ppermute(x, "col", [(i, (i + by) % col) for i in range(col)])

    rows = memory.shape[0] // seq
    total = rows * col
    own = lax.all_to_all(memory.reshape(seq, rows, -1), "seq", 0, 0, tiled=True)

    if pairwise:
        early = far // 2
        late = [d for d in range(far) if d != early]
        kept, left, kept_late, left_late = pair_targets(query, out_grad, me, [[early], late])
        kept, left = cross(kept, swap(left, 2))
        early_qg, own = lax.optimization_barrier((join(kept, [swap(x, 1) for x in left])[0], own))
        early_qg = gather_far(early_qg, early)
        left_late = concat([left_late], after=(own,))
        left_late = swap(left_late, 2)
        kv, *held = project_and_fetch(own, w_key, w_value)
        kept, left = cross(kept_late, left_late, after=(kv,))
        late_qg = join(kept, [swap(x, 1) for x in left])
        for by in range(1, col):
            kv = project(shift(own, by), *held, kv, after=(early_qg, late_qg[0]))
        kv = deal(kv)
        late_qg = [gather_far(x, d) for x, d in zip(late_qg, late)]
        qg = [[late_qg[0], early_qg], late_qg[1:]]
        order = [0, early, *late[1:]]
    else:
        qg = deal(pair_heads(query, out_grad))
        kv = project(own, w_key, w_value)
        for by in range(1, col):
            kv = project(shift(own, by), w_key, w_value, kv)
        kv = deal(kv)
        qg = [by_head(qg, groups)]
    if ranges > 1:
        kv = lax.all_gather(kv, "seq", axis=0, tiled=True, axis_index_groups=same_heads)
    kv = by_head(kv, seq)

    dq, dkv = [], None
    for i, x in enumerate(qg):
        if pairwise:
            x = concat([piece.reshape(-1, 2 * HD) for piece in x], after=(dkv,) * (i > 0))[None]
        weights = (w_key, w_value) if i == len(qg) - 1 else ()
        part, dkv, *weights = attention(x, kv, tgt, dkv, weights)
        dq.append(part)
    w_key, w_value = weights
    dkv = by_owner(dkv, seq)
    if ranges > 1:
        dkv = lax.psum_scatter(dkv, "seq", scatter_dimension=0, tiled=True, axis_index_groups=same_heads)
    dkv = deal(dkv)

    others = [memory_grad(dkv, by * rows, rows, w_key, w_value, seq, BF16) for by in range(1, col)]
    others = [shift(x, col - 1 - i) for i, x in enumerate(others)]
    mine = [memory_grad(dkv, 0, rows, w_key, w_value, seq, F32, (0, 0.125))]
    mine.append(memory_grad(dkv, 0, rows, w_key, w_value, seq, F32, (0.125, 1)))
    if pairwise:
        dq = concat([x.reshape(-1, 2, 2, tgt // 2, 2 * HD) for x in dq], after=mine[:1])
        dq = [gather_far(dq[order.index(d)], d) for d in range(far)]
        summed = add_up(mine, others, after=dq)
        kept, left = part_ways(dq, after=(summed,))
        kept, left = cross(kept, swap(left, 1))
        dq = unpack_query_grad(kept, swap(concat([x[None] for x in left]), 2), me)
    else:
        summed = add_up(mine, others)
        dq = deal(by_owner(dq[0], groups))
        dq = dq.reshape(heads, tgt // 2, 2, HD).transpose(2, 1, 0, 3).reshape(tgt, width)
    d_memory = lax.all_to_all(summed, "seq", 0, 0, tiled=True)
    return dq, d_memory.reshape(memory.shape)


def solution(mesh):
    return jax.shard_map(
        functools.partial(local, mesh.shape["seq"], mesh.shape["col"]),
        mesh=mesh,
        in_specs=(
            P("col", "seq"),
            P("seq", "col"),
            P("seq", "col"),
            P(None, "col"),
            P(None, "col"),
        ),
        out_specs=(P("seq", "col"), P("col", "seq")),
        check_vma=False,
    )
```

profile of v0, /device:TPU:0, one launch (start us, length us, event | category | flops | bytes accessed | tf_op | source)
XLA Modules:
  0.0 145.1 jit_solution(12305185481153325850)
XLA Ops:
  0.6 7.4 %all-to-all-start = ((bf16[16,64,256]{2,1,0:T(8,128)(2,1)}), bf16[16,64,256]{2,1,0:T(8,128)(2,1)S(1)}, u32[]{:S(2)}, u32[]{:S(2)}) async-start(bf16[16,64,256]{2,1,0:T(8,128)(2,1)} %bitcast.41), calls=%async_computation | async-start | bytes 1048576 | tf_op jit(solution)/shard_map/all_to_all | solution.py:444
  10.5 2.0 %collective-permute-start = (bf16[1,2,256,128]{3,2,1,0:T(8,128)(2,1)S(1)}, bf16[1,2,256,128]{3,2,1,0:T(8,128)(2,1)S(1)}, u32[]{:S(2)}, u32[]{:S(2)}) collective-permute-start(bf16[1,2,256,128]{3,2,1,0:T(8,128)(2,1)S(1)} %get-tuple-element.36), channel_id=1, source_target_pairs={{0,4},{2,6},{4,0},{6,2},{8,12},{10,14},{12,8},{14,10},{16,20},{18,... | collective-permute-start | bytes 393224 | tf_op jit(solution)/shard_map/ppermute | solution.py:426
  12.5 5.5 %collective-permute-done.refs_1_ = bf16[1,2,256,128]{3,2,1,0:T(8,128)(2,1)S(1)} collective-permute-done((bf16[1,2,256,128]{3,2,1,0:T(8,128)(2,1)S(1)}, bf16[1,2,256,128]{3,2,1,0:T(8,128)(2,1)S(1)}, u32[]{:S(2)}, u32[]{:S(2)}) %collective-permute-start) | collective-permute-done | bytes 131104 | tf_op jit(solution)/shard_map/ppermute | solution.py:426
  19.5 3.0 %all-to-all-done.refs_1_.m_ref = bf16[16,64,256]{2,1,0:T(8,128)(2,1)S(1)} async-done(((bf16[16,64,256]{2,1,0:T(8,128)(2,1)}), bf16[16,64,256]{2,1,0:T(8,128)(2,1)S(1)}, u32[]{:S(2)}, u32[]{:S(2)}) %all-to-all-start) | async-done | bytes 524320 | tf_op jit(solution)/shard_map/all_to_all | solution.py:444
  23.0 1.5 %collective-permute-start.7 = (bf16[16,64,256]{2,1,0:T(8,128)(2,1)S(1)}, bf16[16,64,256]{2,1,0:T(8,128)(2,1)S(1)}, u32[]{:S(2)}, u32[]{:S(2)}) collective-permute-start(bf16[16,64,256]{2,1,0:T(8,128)(2,1)S(1)} %all-to-all-done.refs_1_.m_ref), channel_id=1, source_target_pairs={{0,1},{1,0},{2,3},{3,2},{4,5},{5,4},{6,7},{7,6},{8,9},{9,8},{10,11... | collective-permute-start | bytes 1572872 | tf_op jit(solution)/shard_map/ppermute | solution.py:440
  24.5 1.9 %collective-permute-start.6 = (bf16[2,2,256,128]{3,2,1,0:T(8,128)(2,1)S(1)}, bf16[2,2,256,128]{3,2,1,0:T(8,128)(2,1)S(1)}, u32[]{:S(2)}, u32[]{:S(2)}) collective-permute-start(bf16[2,2,256,128]{3,2,1,0:T(8,128)(2,1)S(1)} %shard_map.70), channel_id=1, source_target_pairs={{0,16},{2,18},{4,20},{6,22},{8,24},{10,26},{12,28},{14,30},{16,0},... | collective-permute-start | bytes 786440 | tf_op jit(solution)/shard_map/ppermute | solution.py:426
  26.4 6.3 %shard_map.72 = (bf16[16,64,128]{2,1,0:T(8,128)(2,1)S(1)}, bf16[4096,1024]{1,0:T(8,128)(2,1)S(1)}, bf16[4096,1024]{1,0:T(8,128)(2,1)S(1)}) custom-call(bf16[16,64,256]{2,1,0:T(8,128)(2,1)S(1)} %all-to-all-done.refs_1_.m_ref, bf16[4096,1024]{1,0:T(8,128)(2,1)} %refs_1_.3, bf16[4096,1024]{1,0:T(8,128)(2,1)} %refs_2_.3), custom_call_target="tpu_custom_call" | custom-call | flops 1073741824 | bytes 16777216 | tf_op jit(solution)/shard_map/pallas_call | solution.py:207
  35.7 3.8 %collective-permute-done.6.refs_4_ = bf16[2,2,256,128]{3,2,1,0:T(8,128)(2,1)S(1)} collective-permute-done((bf16[2,2,256,128]{3,2,1,0:T(8,128)(2,1)S(1)}, bf16[2,2,256,128]{3,2,1,0:T(8,128)(2,1)S(1)}, u32[]{:S(2)}, u32[]{:S(2)}) %collective-permute-start.6) | collective-permute-done | bytes 262176 | tf_op jit(solution)/shard_map/ppermute | solution.py:426
  39.4 3.9 %shard_map.76 = bf16[16,128,128]{2,1,0:T(8,128)(2,1)} custom-call(bf16[16,64,256]{2,1,0:T(8,128)(2,1)S(1)} %collective-permute-done.7.refs_0_, bf16[4096,1024]{1,0:T(8,128)(2,1)S(1)} %get-tuple-element.47.refs_1_, bf16[4096,1024]{1,0:T(8,128)(2,1)S(1)} %get-tuple-element.48.refs_2_, bf16[16,64,128]{2,1,0:T(8,128)(2,1)S(1)} %get-tuple-element.40.refs_2_.refs_3_, ...), custom_call_target="tpu_custom_call" | custom-call | flops 1073741824 | bytes 17563648 | tf_op jit(solution)/shard_map/pallas_call | solution.py:28
  43.4 3.8 %all-to-all-start.1 = ((bf16[16,128,128]{2,1,0:T(8,128)(2,1)}), bf16[16,128,128]{2,1,0:T(8,128)(2,1)S(1)}, u32[]{:S(2)}, u32[]{:S(2)}) async-start(bf16[16,128,128]{2,1,0:T(8,128)(2,1)} %shard_map.76), calls=%async_computation.1 | async-start | bytes 1048576 | tf_op jit(solution)/shard_map/all_to_all | solution.py:423
  47.1 1.8 %collective-permute-start.8 = (bf16[2,2,256,128]{3,2,1,0:T(8,128)(2,1)S(1)}, bf16[2,2,256,128]{3,2,1,0:T(8,128)(2,1)S(1)}, u32[]{:S(2)}, u32[]{:S(2)}) collective-permute-start(bf16[2,2,256,128]{3,2,1,0:T(8,128)(2,1)S(1)} %get-tuple-element.50), channel_id=1, source_target_pairs={{0,8},{2,10},{4,12},{6,14},{8,0},{10,2},{12,4},{14,6},{16,24},{18,... | collective-permute-start | bytes 786440 | tf_op jit(solution)/shard_map/ppermute | solution.py:426
  49.0 2.4 %collective-permute-start.9 = (bf16[2,2,256,128]{3,2,1,0:T(8,128)(2,1)S(1)}, bf16[2,2,256,128]{3,2,1,0:T(8,128)(2,1)S(1)}, u32[]{:S(2)}, u32[]{:S(2)}) collective-permute-start(bf16[2,2,256,128]{3,2,1,0:T(8,128)(2,1)S(1)} %get-tuple-element.51), channel_id=1, source_target_pairs={{0,24},{2,26},{4,28},{6,30},{8,16},{10,18},{12,20},{14,22},{16,8},... | collective-permute-start | bytes 786440 | tf_op jit(solution)/shard_map/ppermute | solution.py:426
  51.4 10.5 %all-to-all-done.1 = bf16[16,128,128]{2,1,0:T(8,128)(2,1)S(1)} async-done(((bf16[16,128,128]{2,1,0:T(8,128)(2,1)}), bf16[16,128,128]{2,1,0:T(8,128)(2,1)S(1)}, u32[]{:S(2)}, u32[]{:S(2)}) %all-to-all-start.1) | async-done | bytes 524320 | tf_op jit(solution)/shard_map/all_to_all | solution.py:423
  61.8 12.1 %shard_map.77 = (bf16[1,1024,128]{2,1,0:T(8,128)(2,1)S(1)}, f32[1,2048,128]{2,1,0:T(8,128)S(1)}) custom-call(bf16[1,2048,128]{2,1,0:T(8,128)(2,1)S(1)} %bitcast.29, bf16[1,2048,128]{2,1,0:T(8,128)(2,1)S(1)} %bitcast.27), custom_call_target="tpu_custom_call" | custom-call | flops 10737418240 | bytes 4194304 | tf_op jit(solution)/shard_map/pallas_call | solution.py:381
  74.0 12.1 %shard_map.79 = (bf16[1,1024,128]{2,1,0:T(8,128)(2,1)S(1)}, bf16[1,2048,128]{2,1,0:T(8,128)(2,1)S(1)}, bf16[4096,1024]{1,0:T(8,128)(2,1)S(1)}, bf16[4096,1024]{1,0:T(8,128)(2,1)S(1)}) custom-call(bf16[1,2048,128]{2,1,0:T(8,128)(2,1)S(1)} %bitcast.31, bf16[1,2048,128]{2,1,0:T(8,128)(2,1)S(1)} %bitcast.28, ...), custom_call_target="tpu_custom_call" | custom-call | flops 10737418240 | bytes 4194304 | tf_op jit(solution)/shard_map/pallas_call | solution.py:381
  86.1 18.3 %all_to_all.20.refs_0_ = bf16[16,128,128]{2,1,0:T(8,128)(2,1)S(1)} all-to-all(bf16[16,128,128]{2,1,0:T(8,128)(2,1)S(1)} %bitcast.30), channel_id=1, replica_groups={{0,2,4,6,8,10,12,14,16,18,20,22,24,26,28,30},{1,3,5,7,9,11,13,15,17,19,..., dimensions={0} | all-to-all | bytes 1048576 | tf_op jit(solution)/shard_map/all_to_all | solution.py:423
  104.5 4.6 %shard_map.83 = bf16[16,64,256]{2,1,0:T(8,128)(2,1)S(1)} custom-call(bf16[16,128,128]{2,1,0:T(8,128)(2,1)S(1)} %all_to_all.20.refs_0_, bf16[4096,1024]{1,0:T(8,128)(2,1)S(1)} %get-tuple-element.55.refs_1_, bf16[4096,1024]{1,0:T(8,128)(2,1)S(1)} %get-tuple-element.56.refs_2_), custom_call_target="tpu_custom_call" | custom-call | flops 1073741824 | bytes 17301504 | tf_op jit(solution)/shard_map/pallas_call | solution.py:28
  110.6 1.4 collective-permute-start.12
  113.2 1.8 %collective-permute-start.10 = (bf16[2,2,128,128]{3,2,1,0:T(8,128)(2,1)S(1)}, bf16[2,2,128,128]{3,2,1,0:T(8,128)(2,1)S(1)}, u32[]{:S(2)}, u32[]{:S(2)}) collective-permute-start(bf16[2,2,128,128]{3,2,1,0:T(8,128)(2,1)S(1)} %get-tuple-element.66), channel_id=1, source_target_pairs={{0,8},{2,10},{4,12},{6,14},{8,0},{10,2},{12,4},{14,6},{16,24},{18,... | collective-permute-start | bytes 393224 | tf_op jit(solution)/shard_map/ppermute | solution.py:426
  115.0 4.1 %shard_map.82.refs_1_ = f32[14,64,256]{2,1,0:T(8,128)S(1)} custom-call(bf16[16,128,128]{2,1,0:T(8,128)(2,1)S(1)} %all_to_all.20.refs_0_, bf16[4096,1024]{1,0:T(8,128)(2,1)S(1)} %get-tuple-element.55.refs_1_, bf16[4096,1024]{1,0:T(8,128)(2,1)S(1)} %get-tuple-element.56.refs_2_), custom_call_target="tpu_custom_call" | custom-call | flops 939524096 | bytes 17301504 | tf_op jit(solution)/shard_map/pallas_call | solution.py:28
  119.1 6.3 %collective-permute-done.11.refs_5_.refs_2_ = bf16[2,2,128,128]{3,2,1,0:T(8,128)(2,1)S(1)} collective-permute-done((bf16[2,2,128,128]{3,2,1,0:T(8,128)(2,1)S(1)}, bf16[2,2,128,128]{3,2,1,0:T(8,128)(2,1)S(1)}, u32[]{:S(2)}, u32[]{:S(2)}) %collective-permute-start.11) | collective-permute-done | bytes 131104 | tf_op jit(solution)/shard_map/ppermute | solution.py:426
  126.3 3.6 %all-to-all-start.3 = ((bf16[16,64,256]{2,1,0:T(8,128)(2,1)}), bf16[16,64,256]{2,1,0:T(8,128)(2,1)S(1)}, u32[]{:S(2)}, u32[]{:S(2)}) async-start(bf16[16,64,256]{2,1,0:T(8,128)(2,1)} %shard_map.84.refs_4_), calls=%async_computation.3 | async-start | bytes 1048576 | tf_op jit(solution)/shard_map/all_to_all | solution.py:503
  131.6 1.9 %collective-permute-start.15 = (bf16[4,2,128,128]{3,2,1,0:T(8,128)(2,1)S(1)}, bf16[4,2,128,128]{3,2,1,0:T(8,128)(2,1)S(1)}, u32[]{:S(2)}, u32[]{:S(2)}) collective-permute-start(bf16[4,2,128,128]{3,2,1,0:T(8,128)(2,1)S(1)} %shard_map.87), channel_id=1, source_target_pairs={{0,4},{2,6},{4,0},{6,2},{8,12},{10,14},{12,8},{14,10},{16,20},{18,... | collective-permute-start | bytes 786440 | tf_op jit(solution)/shard_map/ppermute | solution.py:426
  133.5 9.7 %collective-permute-done.15.refs_2_ = bf16[4,2,128,128]{3,2,1,0:T(8,128)(2,1)S(1)} collective-permute-done((bf16[4,2,128,128]{3,2,1,0:T(8,128)(2,1)S(1)}, bf16[4,2,128,128]{3,2,1,0:T(8,128)(2,1)S(1)}, u32[]{:S(2)}, u32[]{:S(2)}) %collective-permute-start.15) | collective-permute-done | bytes 262176 | tf_op jit(solution)/shard_map/ppermute | solution.py:426
  (42 shorter events, 14.7 us)
Async XLA Ops:
  0.6 21.9 %all-to-all-start = ((bf16[16,64,256]{2,1,0:T(8,128)(2,1)}), bf16[16,64,256]{2,1,0:T(8,128)(2,1)S(1)}, u32[]{:S(2)}, u32[]{:S(2)}) async-start(bf16[16,64,256]{2,1,0:T(8,128)(2,1)} %bitcast.41), calls=%async_computation | async-start | bytes 1048576 | tf_op jit(solution)/shard_map/all_to_all | solution.py:444
  8.0 1.0 copy-start
  9.1 1.0 copy-start.1
  10.5 7.5 %collective-permute-start = (bf16[1,2,256,128]{3,2,1,0:T(8,128)(2,1)S(1)}, bf16[1,2,256,128]{3,2,1,0:T(8,128)(2,1)S(1)}, u32[]{:S(2)}, u32[]{:S(2)}) collective-permute-start(bf16[1,2,256,128]{3,2,1,0:T(8,128)(2,1)S(1)} %get-tuple-element.36), channel_id=1, source_target_pairs={{0,4},{2,6},{4,0},{6,2},{8,12},{10,14},{12,8},{14,10},{16,20},{18,... | collective-permute-start | bytes 393224 | tf_op jit(solution)/shard_map/ppermute | solution.py:426
  18.0 1.4 collective-permute-start.1
  22.5 11.1 %collective-permute-start.2 = (bf16[3,2,256,128]{3,2,1,0:T(8,128)(2,1)S(1)}, bf16[3,2,256,128]{3,2,1,0:T(8,128)(2,1)S(1)}, u32[]{:S(2)}, u32[]{:S(2)}) collective-permute-start(bf16[3,2,256,128]{3,2,1,0:T(8,128)(2,1)S(1)} %shard_map.71), channel_id=1, source_target_pairs={{0,4},{2,6},{4,0},{6,2},{8,12},{10,14},{12,8},{14,10},{16,20},{18,... | collective-permute-start | bytes 1179656 | tf_op jit(solution)/shard_map/ppermute | solution.py:426
  23.0 16.4 %collective-permute-start.7 = (bf16[16,64,256]{2,1,0:T(8,128)(2,1)S(1)}, bf16[16,64,256]{2,1,0:T(8,128)(2,1)S(1)}, u32[]{:S(2)}, u32[]{:S(2)}) collective-permute-start(bf16[16,64,256]{2,1,0:T(8,128)(2,1)S(1)} %all-to-all-done.refs_1_.m_ref), channel_id=1, source_target_pairs={{0,1},{1,0},{2,3},{3,2},{4,5},{5,4},{6,7},{7,6},{8,9},{9,8},{10,11... | collective-permute-start | bytes 1572872 | tf_op jit(solution)/shard_map/ppermute | solution.py:440
  24.5 14.9 %collective-permute-start.6 = (bf16[2,2,256,128]{3,2,1,0:T(8,128)(2,1)S(1)}, bf16[2,2,256,128]{3,2,1,0:T(8,128)(2,1)S(1)}, u32[]{:S(2)}, u32[]{:S(2)}) collective-permute-start(bf16[2,2,256,128]{3,2,1,0:T(8,128)(2,1)S(1)} %shard_map.70), channel_id=1, source_target_pairs={{0,16},{2,18},{4,20},{6,22},{8,24},{10,26},{12,28},{14,30},{16,0},... | collective-permute-start | bytes 786440 | tf_op jit(solution)/shard_map/ppermute | solution.py:426
  33.7 1.4 collective-permute-start.3
  33.8 1.5 %collective-permute-start.4 = (bf16[2,256,128]{2,1,0:T(8,128)(2,1)S(1)}, bf16[2,256,128]{2,1,0:T(8,128)(2,1)S(1)}, u32[]{:S(2)}, u32[]{:S(2)}) collective-permute-start(bf16[2,256,128]{2,1,0:T(8,128)(2,1)S(1)} %get-tuple-element.43), channel_id=1, source_target_pairs={{0,2},{2,0},{4,6},{6,4},{8,10},{10,8},{12,14},{14,12},{16,18},{18,... | collective-permute-start | bytes 393224 | tf_op jit(solution)/shard_map/ppermute | solution.py:426
  34.3 1.3 collective-permute-start.5
  43.4 18.5 %all-to-all-start.1 = ((bf16[16,128,128]{2,1,0:T(8,128)(2,1)}), bf16[16,128,128]{2,1,0:T(8,128)(2,1)S(1)}, u32[]{:S(2)}, u32[]{:S(2)}) async-start(bf16[16,128,128]{2,1,0:T(8,128)(2,1)} %shard_map.76), calls=%async_computation.1 | async-start | bytes 1048576 | tf_op jit(solution)/shard_map/all_to_all | solution.py:423
  47.1 26.8 %collective-permute-start.8 = (bf16[2,2,256,128]{3,2,1,0:T(8,128)(2,1)S(1)}, bf16[2,2,256,128]{3,2,1,0:T(8,128)(2,1)S(1)}, u32[]{:S(2)}, u32[]{:S(2)}) collective-permute-start(bf16[2,2,256,128]{3,2,1,0:T(8,128)(2,1)S(1)} %get-tuple-element.50), channel_id=1, source_target_pairs={{0,8},{2,10},{4,12},{6,14},{8,0},{10,2},{12,4},{14,6},{16,24},{18,... | collective-permute-start | bytes 786440 | tf_op jit(solution)/shard_map/ppermute | solution.py:426
  49.0 25.0 %collective-permute-start.9 = (bf16[2,2,256,128]{3,2,1,0:T(8,128)(2,1)S(1)}, bf16[2,2,256,128]{3,2,1,0:T(8,128)(2,1)S(1)}, u32[]{:S(2)}, u32[]{:S(2)}) collective-permute-start(bf16[2,2,256,128]{3,2,1,0:T(8,128)(2,1)S(1)} %get-tuple-element.51), channel_id=1, source_target_pairs={{0,24},{2,26},{4,28},{6,30},{8,16},{10,18},{12,20},{14,22},{16,8},... | collective-permute-start | bytes 786440 | tf_op jit(solution)/shard_map/ppermute | solution.py:426
  109.1 16.3 %collective-permute-start.13 = (bf16[16,64,256]{2,1,0:T(8,128)(2,1)S(1)}, bf16[16,64,256]{2,1,0:T(8,128)(2,1)S(1)}, u32[]{:S(2)}, u32[]{:S(2)}) collective-permute-start(bf16[16,64,256]{2,1,0:T(8,128)(2,1)S(1)} %shard_map.83), channel_id=1, source_target_pairs={{0,1},{1,0},{2,3},{3,2},{4,5},{5,4},{6,7},{7,6},{8,9},{9,8},{10,11... | collective-permute-start | bytes 1572872 | tf_op jit(solution)/shard_map/ppermute | solution.py:440
  110.6 8.5 %collective-permute-start.12 = (bf16[2,2,128,128]{3,2,1,0:T(8,128)(2,1)S(1)}, bf16[2,2,128,128]{3,2,1,0:T(8,128)(2,1)S(1)}, u32[]{:S(2)}, u32[]{:S(2)}) collective-permute-start(bf16[2,2,128,128]{3,2,1,0:T(8,128)(2,1)S(1)} %get-tuple-element.64), channel_id=1, source_target_pairs={{0,24},{2,26},{4,28},{6,30},{8,16},{10,18},{12,20},{14,22},{16,8},... | collective-permute-start | bytes 393224 | tf_op jit(solution)/shard_map/ppermute | solution.py:426
  112.0 13.4 %collective-permute-start.11 = (bf16[2,2,128,128]{3,2,1,0:T(8,128)(2,1)S(1)}, bf16[2,2,128,128]{3,2,1,0:T(8,128)(2,1)S(1)}, u32[]{:S(2)}, u32[]{:S(2)}) collective-permute-start(bf16[2,2,128,128]{3,2,1,0:T(8,128)(2,1)S(1)} %get-tuple-element.65), channel_id=1, source_target_pairs={{0,16},{2,18},{4,20},{6,22},{8,24},{10,26},{12,28},{14,30},{16,0},... | collective-permute-start | bytes 393224 | tf_op jit(solution)/shard_map/ppermute | solution.py:426
  113.2 12.2 %collective-permute-start.10 = (bf16[2,2,128,128]{3,2,1,0:T(8,128)(2,1)S(1)}, bf16[2,2,128,128]{3,2,1,0:T(8,128)(2,1)S(1)}, u32[]{:S(2)}, u32[]{:S(2)}) collective-permute-start(bf16[2,2,128,128]{3,2,1,0:T(8,128)(2,1)S(1)} %get-tuple-element.66), channel_id=1, source_target_pairs={{0,8},{2,10},{4,12},{6,14},{8,0},{10,2},{12,4},{14,6},{16,24},{18,... | collective-permute-start | bytes 393224 | tf_op jit(solution)/shard_map/ppermute | solution.py:426
  126.3 18.0 %all-to-all-start.3 = ((bf16[16,64,256]{2,1,0:T(8,128)(2,1)}), bf16[16,64,256]{2,1,0:T(8,128)(2,1)S(1)}, u32[]{:S(2)}, u32[]{:S(2)}) async-start(bf16[16,64,256]{2,1,0:T(8,128)(2,1)} %shard_map.84.refs_4_), calls=%async_computation.3 | async-start | bytes 1048576 | tf_op jit(solution)/shard_map/all_to_all | solution.py:503
  129.9 1.6 %collective-permute-start.14 = (bf16[4,2,128,128]{3,2,1,0:T(8,128)(2,1)S(1)}, bf16[4,2,128,128]{3,2,1,0:T(8,128)(2,1)S(1)}, u32[]{:S(2)}, u32[]{:S(2)}) collective-permute-start(bf16[4,2,128,128]{3,2,1,0:T(8,128)(2,1)S(1)} %get-tuple-element.58), channel_id=1, source_target_pairs={{0,2},{2,0},{4,6},{6,4},{8,10},{10,8},{12,14},{14,12},{16,18},{18,... | collective-permute-start | bytes 786440 | tf_op jit(solution)/shard_map/ppermute | solution.py:426
  131.6 11.5 %collective-permute-start.15 = (bf16[4,2,128,128]{3,2,1,0:T(8,128)(2,1)S(1)}, bf16[4,2,128,128]{3,2,1,0:T(8,128)(2,1)S(1)}, u32[]{:S(2)}, u32[]{:S(2)}) collective-permute-start(bf16[4,2,128,128]{3,2,1,0:T(8,128)(2,1)S(1)} %shard_map.87), channel_id=1, source_target_pairs={{0,4},{2,6},{4,0},{6,2},{8,12},{10,14},{12,8},{14,10},{16,20},{18,... | collective-permute-start | bytes 786440 | tf_op jit(solution)/shard_map/ppermute | solution.py:426
where the time goes:
time: 146 us; the launch traced here: 145 us
  Pallas kernels  46.7 us (32%)
  waiting for transfers between devices  43.6 us (30%)
  starting transfers between devices  32.8 us (22%)
  blocking collectives  18.3 us (13%)
  local copies, waits for them, and re-layouts  2.91 us (2%)
    ppermute x14, waiting for transfers between devices, swap(): return lax.ppermute(x, 'seq', [(i, i ^ bits) for i in range(seq)])  29.9 us
    pallas_call x2, Pallas kernels, attention(): pl.pallas_call(functools.partial(attention_kernel, tile, math.gcd(src, ch...  24.2 us
    all_to_all x1, blocking collectives, deal(): lax.all_to_all(x, 'seq', 0, 0, tiled=True, axis_index_groups=same_range)  18.3 us
    pallas_call x18, Pallas kernels, whole(): pl.pallas_call(lambda *refs: kernel(*refs[:n], *refs[n + len(after):]), i...  16.1 us
    ppermute x14, starting transfers between devices, swap(): return lax.ppermute(x, 'seq', [(i, i ^ bits) for i in range(seq)])  16 us
    all_to_all x1, waiting for transfers between devices, deal(): lax.all_to_all(x, 'seq', 0, 0, tiled=True, axis_index_groups=same_range)  10.5 us
    all_to_all x1, starting transfers between devices, local(): own = lax.all_to_all(memory.reshape(seq, rows, -1), 'seq', 0, 0, tiled=True)  7.4 us
    pallas_call x1, Pallas kernels, project_and_fetch(): pl.pallas_call(kernel, in_specs=[VMEM, anywhere, anywhere], out_specs=[VM...  6.31 us
  transfers between devices with their start and end apart: 19, of which 13 were waited for; matrix products, arithmetic and copies ran while one was open for 0% of the time, Pallas kernels for 17%

commit v1 on v0

--- a/solution.py
+++ b/solution.py
@@ -225,19 +225,20 @@
     )(mem, *[pltpu.with_memory_space_constraint(w, pltpu.MemorySpace.HBM) for w in (w_key, w_value)])
 
 
-def add_up(parts, others, after=()):
-    def kernel(*refs):
-        out_ref, at = refs[-1], 0
-        for ref in refs[: len(parts)]:
-            here = pl.ds(at, ref.shape[0])
-            total = ref[...]
-            for other in refs[len(parts) : -1]:
-                total = total + other[here].astype(F32)
+def add_up(mine, others, after=()):
+    half = mine.shape[0] // 2
+
+    def kernel(mine_ref, *refs):
+        out_ref = refs[-1]
+        for i in range(2):
+            here = pl.ds(i * half, half)
+            total = mine_ref[here]
+            for ref in refs[i:-1:2]:
+                total = total + ref[...].astype(F32)
             out_ref[here] = total.astype(BF16)
-            at += ref.shape[0]
-
-    out = [jax.ShapeDtypeStruct((sum(x.shape[0] for x in parts), *parts[0].shape[1:]), BF16)]
-    return whole(kernel, out, *parts, *others, after=after)[0]
+
+    out = [jax.ShapeDtypeStruct(mine.shape, BF16)]
+    return whole(kernel, out, mine, *others, after=after)[0]
 
 
 def unpack_query_grad(kept, came, me):
@@ -456,11 +457,11 @@
         kept, left = cross(kept_late, left_late, after=(kv,))
         late_qg = join(kept, [swap(x, 1) for x in left])
         for by in range(1, col):
-            kv = project(shift(own, by), *held, kv, after=(early_qg, late_qg[0]))
+            kv = project(shift(own, by), *held, kv, after=(late_qg[0],))
+        early_qg, kv = lax.optimization_barrier((early_qg, kv))
         kv = deal(kv)
         late_qg = [gather_far(x, d) for x, d in zip(late_qg, late)]
         qg = [[late_qg[0], early_qg], late_qg[1:]]
-        order = [0, early, *late[1:]]
     else:
         qg = deal(pair_heads(query, out_grad))
         kv = project(own, w_key, w_value)
@@ -479,19 +480,29 @@
         weights = (w_key, w_value) if i == len(qg) - 1 else ()
         part, dkv, *weights = attention(x, kv, tgt, dkv, weights)
         dq.append(part)
+        if pairwise and i == 0:
+            home, away = dq.pop().reshape(2, 2, 2, tgt // 2, 2 * HD)
+            away = gather_far(away, early)
     w_key, w_value = weights
+    if pairwise:
+        dkv, away = lax.optimization_barrier((dkv, away))
     dkv = by_owner(dkv, seq)
     if ranges > 1:
         dkv = lax.psum_scatter(dkv, "seq", scatter_dimension=0, tiled=True, axis_index_groups=same_heads)
     dkv = deal(dkv)
 
-    others = [memory_grad(dkv, by * rows, rows, w_key, w_value, seq, BF16) for by in range(1, col)]
-    others = [shift(x, col - 1 - i) for i, x in enumerate(others)]
-    mine = [memory_grad(dkv, 0, rows, w_key, w_value, seq, F32, (0, 0.125))]
-    mine.append(memory_grad(dkv, 0, rows, w_key, w_value, seq, F32, (0.125, 1)))
+    others = [
+        (by, memory_grad(dkv, by * rows, rows, w_key, w_value, seq, BF16, span))
+        for by in range(1, col)
+        for span in ((0, 0.5), (0.5, 1))
+    ]
+    first = [x for _, x in others]
+    others = [shift(x, col - by) for by, x in others]
+    mine = memory_grad(dkv, 0, rows, w_key, w_value, seq, F32)
     if pairwise:
-        dq = concat([x.reshape(-1, 2, 2, tgt // 2, 2 * HD) for x in dq], after=mine[:1])
-        dq = [gather_far(dq[order.index(d)], d) for d in range(far)]
+        dq = concat([x.reshape(-1, 2, 2, tgt // 2, 2 * HD) for x in dq], after=first)
+        dq = [home, *[gather_far(x, d) for x, d in zip(dq, late[1:])]]
+        dq.insert(early, away)
         summed = add_up(mine, others, after=dq)
         kept, left = part_ways(dq, after=(summed,))
         kept, left = cross(kept, swap(left, 1))

time: 146 us -> 142 us (0.973)
  waiting for transfers between devices: 43.6 us -> 37.2 us
  starting transfers between devices: 32.8 us -> 36.2 us
    ppermute x14, waiting for transfers between devices: 29.9 us -> 22.1 us  [swap(): return lax.ppermute(x, 'seq', [(i, i ^ bits) for i in range(seq)])]
    ppermute x2 -> x3, waiting for transfers between devices: 0.01 us -> 1.65 us  [shift(): return lax.ppermute(x, 'col', [(i, (i + by) % col) for i in range(col)])]
    ppermute x2 -> x3, starting transfers between devices: 2.09 us -> 3.65 us  [shift(): return lax.ppermute(x, 'col', [(i, (i + by) % col) for i in range(col)])]
  transfers between devices with their start and end apart: 19 -> 20, of which waited for: 13 -> 13; matrix products, arithmetic and copies ran while one was open for 0% -> 0% of each run, Pallas kernels for 17% -> 31%
where the time goes in v1:
time: 142 us; the launch traced here: 141 us
  Pallas kernels  46.7 us (33%)
  waiting for transfers between devices  37.2 us (26%)
  starting transfers between devices  36.2 us (25%)
  blocking collectives  17.6 us (12%)
  local copies, waits for them, and re-layouts  2.91 us (2%)
    pallas_call x2, Pallas kernels, attention(): pl.pallas_call(functools.partial(attention_kernel, tile, math.gcd(src, ch...  24.2 us
    ppermute x14, waiting for transfers between devices, swap(): return lax.ppermute(x, 'seq', [(i, i ^ bits) for i in range(seq)])  22.1 us
    all_to_all x1, blocking collectives, deal(): lax.all_to_all(x, 'seq', 0, 0, tiled=True, axis_index_groups=same_range)  17.6 us
    ppermute x14, starting transfers between devices, swap(): return lax.ppermute(x, 'seq', [(i, i ^ bits) for i in range(seq)])  17.1 us
    pallas_call x18, Pallas kernels, whole(): pl.pallas_call(lambda *refs: kernel(*refs[:n], *refs[n + len(after):]), i...  16.1 us
    all_to_all x1, waiting for transfers between devices, deal(): lax.all_to_all(x, 'seq', 0, 0, tiled=True, axis_index_groups=same_range)  10.5 us
    all_to_all x1, starting transfers between devices, local(): own = lax.all_to_all(memory.reshape(seq, rows, -1), 'seq', 0, 0, tiled=True)  7.4 us
    pallas_call x1, Pallas kernels, project_and_fetch(): pl.pallas_call(kernel, in_specs=[VMEM, anywhere, anywhere], out_specs=[VM...  6.31 us
  transfers between devices with their start and end apart: 20, of which 13 were waited for; matrix products, arithmetic and copies ran while one was open for 0% of the time, Pallas kernels for 31%

profile of v1, /device:TPU:0, one launch (start us, length us, event | category | flops | bytes accessed | tf_op | source)
XLA Modules:
  0.0 141.3 jit_solution(2327195382575641776)
XLA Ops:
  0.6 7.4 %all-to-all-start = ((bf16[16,64,256]{2,1,0:T(8,128)(2,1)}), bf16[16,64,256]{2,1,0:T(8,128)(2,1)S(1)}, u32[]{:S(2)}, u32[]{:S(2)}) async-start(bf16[16,64,256]{2,1,0:T(8,128)(2,1)} %bitcast.39), calls=%async_computation | async-start | bytes 1048576 | tf_op jit(solution)/shard_map/all_to_all | solution.py:445
  10.5 2.0 %collective-permute-start = (bf16[1,2,256,128]{3,2,1,0:T(8,128)(2,1)S(1)}, bf16[1,2,256,128]{3,2,1,0:T(8,128)(2,1)S(1)}, u32[]{:S(2)}, u32[]{:S(2)}) collective-permute-start(bf16[1,2,256,128]{3,2,1,0:T(8,128)(2,1)S(1)} %get-tuple-element.40), channel_id=1, source_target_pairs={{0,4},{2,6},{4,0},{6,2},{8,12},{10,14},{12,8},{14,10},{16,20},{18,... | collective-permute-start | bytes 393224 | tf_op jit(solution)/shard_map/ppermute | solution.py:427
  12.5 5.5 %collective-permute-done.refs_1_ = bf16[1,2,256,128]{3,2,1,0:T(8,128)(2,1)S(1)} collective-permute-done((bf16[1,2,256,128]{3,2,1,0:T(8,128)(2,1)S(1)}, bf16[1,2,256,128]{3,2,1,0:T(8,128)(2,1)S(1)}, u32[]{:S(2)}, u32[]{:S(2)}) %collective-permute-start) | collective-permute-done | bytes 131104 | tf_op jit(solution)/shard_map/ppermute | solution.py:427
  19.5 3.0 %all-to-all-done.refs_1_.m_ref = bf16[16,64,256]{2,1,0:T(8,128)(2,1)S(1)} async-done(((bf16[16,64,256]{2,1,0:T(8,128)(2,1)}), bf16[16,64,256]{2,1,0:T(8,128)(2,1)S(1)}, u32[]{:S(2)}, u32[]{:S(2)}) %all-to-all-start) | async-done | bytes 524320 | tf_op jit(solution)/shard_map/all_to_all | solution.py:445
  23.0 1.5 %collective-permute-start.7 = (bf16[16,64,256]{2,1,0:T(8,128)(2,1)S(1)}, bf16[16,64,256]{2,1,0:T(8,128)(2,1)S(1)}, u32[]{:S(2)}, u32[]{:S(2)}) collective-permute-start(bf16[16,64,256]{2,1,0:T(8,128)(2,1)S(1)} %all-to-all-done.refs_1_.m_ref), channel_id=1, source_target_pairs={{0,1},{1,0},{2,3},{3,2},{4,5},{5,4},{6,7},{7,6},{8,9},{9,8},{10,11... | collective-permute-start | bytes 1572872 | tf_op jit(solution)/shard_map/ppermute | solution.py:441
  24.5 1.9 %collective-permute-start.6 = (bf16[2,2,256,128]{3,2,1,0:T(8,128)(2,1)S(1)}, bf16[2,2,256,128]{3,2,1,0:T(8,128)(2,1)S(1)}, u32[]{:S(2)}, u32[]{:S(2)}) collective-permute-start(bf16[2,2,256,128]{3,2,1,0:T(8,128)(2,1)S(1)} %shard_map.70), channel_id=1, source_target_pairs={{0,16},{2,18},{4,20},{6,22},{8,24},{10,26},{12,28},{14,30},{16,0},... | collective-permute-start | bytes 786440 | tf_op jit(solution)/shard_map/ppermute | solution.py:427
  26.4 6.3 %shard_map.72 = (bf16[16,64,128]{2,1,0:T(8,128)(2,1)S(1)}, bf16[4096,1024]{1,0:T(8,128)(2,1)S(1)}, bf16[4096,1024]{1,0:T(8,128)(2,1)S(1)}) custom-call(bf16[16,64,256]{2,1,0:T(8,128)(2,1)S(1)} %all-to-all-done.refs_1_.m_ref, bf16[4096,1024]{1,0:T(8,128)(2,1)} %refs_1_.3, bf16[4096,1024]{1,0:T(8,128)(2,1)} %refs_2_.3), custom_call_target="tpu_custom_call" | custom-call | flops 1073741824 | bytes 16777216 | tf_op jit(solution)/shard_map/pallas_call | solution.py:207
  35.7 1.6 %collective-permute-done.7.refs_0_ = bf16[16,64,256]{2,1,0:T(8,128)(2,1)S(1)} collective-permute-done((bf16[16,64,256]{2,1,0:T(8,128)(2,1)S(1)}, bf16[16,64,256]{2,1,0:T(8,128)(2,1)S(1)}, u32[]{:S(2)}, u32[]{:S(2)}) %collective-permute-start.7) | collective-permute-done | bytes 524320 | tf_op jit(solution)/shard_map/ppermute | solution.py:441
  37.3 3.9 %shard_map.75 = bf16[16,128,128]{2,1,0:T(8,128)(2,1)} custom-call(bf16[16,64,256]{2,1,0:T(8,128)(2,1)S(1)} %collective-permute-done.7.refs_0_, bf16[4096,1024]{1,0:T(8,128)(2,1)S(1)} %get-tuple-element.51.refs_1_, bf16[4096,1024]{1,0:T(8,128)(2,1)S(1)} %get-tuple-element.52.refs_2_, bf16[16,64,128]{2,1,0:T(8,128)(2,1)S(1)} %get-tuple-element.44.refs_2_.refs_3_, ...), custom_call_target="tpu_custom_call" | custom-call | flops 1073741824 | bytes 17563648 | tf_op jit(solution)/shard_map/pallas_call | solution.py:28
  41.2 3.8 %all-to-all-start.1 = ((bf16[16,128,128]{2,1,0:T(8,128)(2,1)}), bf16[16,128,128]{2,1,0:T(8,128)(2,1)S(1)}, u32[]{:S(2)}, u32[]{:S(2)}) async-start(bf16[16,128,128]{2,1,0:T(8,128)(2,1)} %shard_map.75), calls=%async_computation.1 | async-start | bytes 1048576 | tf_op jit(solution)/shard_map/all_to_all | solution.py:424
  45.1 2.0 %collective-permute-start.8 = (bf16[2,2,256,128]{3,2,1,0:T(8,128)(2,1)S(1)}, bf16[2,2,256,128]{3,2,1,0:T(8,128)(2,1)S(1)}, u32[]{:S(2)}, u32[]{:S(2)}) collective-permute-start(bf16[2,2,256,128]{3,2,1,0:T(8,128)(2,1)S(1)} %get-tuple-element.56), channel_id=1, source_target_pairs={{0,8},{2,10},{4,12},{6,14},{8,0},{10,2},{12,4},{14,6},{16,24},{18,... | collective-permute-start | bytes 786440 | tf_op jit(solution)/shard_map/ppermute | solution.py:427
  47.0 2.4 %collective-permute-start.9 = (bf16[2,2,256,128]{3,2,1,0:T(8,128)(2,1)S(1)}, bf16[2,2,256,128]{3,2,1,0:T(8,128)(2,1)S(1)}, u32[]{:S(2)}, u32[]{:S(2)}) collective-permute-start(bf16[2,2,256,128]{3,2,1,0:T(8,128)(2,1)S(1)} %get-tuple-element.57), channel_id=1, source_target_pairs={{0,24},{2,26},{4,28},{6,30},{8,16},{10,18},{12,20},{14,22},{16,8},... | collective-permute-start | bytes 786440 | tf_op jit(solution)/shard_map/ppermute | solution.py:427
  49.4 10.5 %all-to-all-done.1 = bf16[16,128,128]{2,1,0:T(8,128)(2,1)S(1)} async-done(((bf16[16,128,128]{2,1,0:T(8,128)(2,1)}), bf16[16,128,128]{2,1,0:T(8,128)(2,1)S(1)}, u32[]{:S(2)}, u32[]{:S(2)}) %all-to-all-start.1) | async-done | bytes 524320 | tf_op jit(solution)/shard_map/all_to_all | solution.py:424
  59.9 12.1 %shard_map.77 = (bf16[1,1024,128]{2,1,0:T(8,128)(2,1)S(1)}, f32[1,2048,128]{2,1,0:T(8,128)S(1)}) custom-call(bf16[1,2048,128]{2,1,0:T(8,128)(2,1)S(1)} %bitcast.28, bf16[1,2048,128]{2,1,0:T(8,128)(2,1)S(1)} %bitcast.25), custom_call_target="tpu_custom_call" | custom-call | flops 10737418240 | bytes 4194304 | tf_op jit(solution)/shard_map/pallas_call | solution.py:382
  72.0 2.3 %collective-permute-start.10 = (bf16[2,2,128,128]{3,2,1,0:T(8,128)(2,1)S(1)}, bf16[2,2,128,128]{3,2,1,0:T(8,128)(2,1)S(1)}, u32[]{:S(2)}, u32[]{:S(2)}) collective-permute-start(bf16[2,2,128,128]{3,2,1,0:T(8,128)(2,1)S(1)} %bitcast.40), channel_id=1, source_target_pairs={{0,16},{2,18},{4,20},{6,22},{8,24},{10,26},{12,28},{14,30},{16,0},... | collective-permute-start | bytes 393224 | tf_op jit(solution)/shard_map/ppermute | solution.py:427
  74.4 12.1 %shard_map.79 = (bf16[1,1024,128]{2,1,0:T(8,128)(2,1)S(1)}, bf16[1,2048,128]{2,1,0:T(8,128)(2,1)S(1)}, bf16[4096,1024]{1,0:T(8,128)(2,1)S(1)}, bf16[4096,1024]{1,0:T(8,128)(2,1)S(1)}) custom-call(bf16[1,2048,128]{2,1,0:T(8,128)(2,1)S(1)} %bitcast.29, bf16[1,2048,128]{2,1,0:T(8,128)(2,1)S(1)} %bitcast.26, ...), custom_call_target="tpu_custom_call" | custom-call | flops 10737418240 | bytes 4194304 | tf_op jit(solution)/shard_map/pallas_call | solution.py:382
  86.5 17.6 %all_to_all.20.refs_0_ = bf16[16,128,128]{2,1,0:T(8,128)(2,1)S(1)} all-to-all(bf16[16,128,128]{2,1,0:T(8,128)(2,1)S(1)} %bitcast.27), channel_id=1, replica_groups={{0,2,4,6,8,10,12,14,16,18,20,22,24,26,28,30},{1,3,5,7,9,11,13,15,17,19,..., dimensions={0} | all-to-all | bytes 1048576 | tf_op jit(solution)/shard_map/all_to_all | solution.py:424
  104.1 2.5 %shard_map.80.refs_1_ = bf16[8,64,256]{2,1,0:T(8,128)(2,1)S(1)} custom-call(bf16[16,128,128]{2,1,0:T(8,128)(2,1)S(1)} %all_to_all.20.refs_0_, bf16[4096,1024]{1,0:T(8,128)(2,1)S(1)} %get-tuple-element.62.refs_1_, bf16[4096,1024]{1,0:T(8,128)(2,1)S(1)} %get-tuple-element.63.refs_2_), custom_call_target="tpu_custom_call" | custom-call | flops 536870912 | bytes 17301504 | tf_op jit(solution)/shard_map/pallas_call | solution.py:28
  106.6 1.6 %collective-permute-start.13 = (bf16[8,64,256]{2,1,0:T(8,128)(2,1)S(1)}, bf16[8,64,256]{2,1,0:T(8,128)(2,1)S(1)}, u32[]{:S(2)}, u32[]{:S(2)}) collective-permute-start(bf16[8,64,256]{2,1,0:T(8,128)(2,1)S(1)} %shard_map.80.refs_1_), channel_id=1, source_target_pairs={{0,1},{1,0},{2,3},{3,2},{4,5},{5,4},{6,7},{7,6},{8,9},{9,8},{10,11... | collective-permute-start | bytes 786440 | tf_op jit(solution)/shard_map/ppermute | solution.py:441
  108.1 2.5 %shard_map.81.refs_2_ = bf16[8,64,256]{2,1,0:T(8,128)(2,1)S(1)} custom-call(bf16[16,128,128]{2,1,0:T(8,128)(2,1)S(1)} %all_to_all.20.refs_0_, bf16[4096,1024]{1,0:T(8,128)(2,1)S(1)} %get-tuple-element.62.refs_1_, bf16[4096,1024]{1,0:T(8,128)(2,1)S(1)} %get-tuple-element.63.refs_2_), custom_call_target="tpu_custom_call" | custom-call | flops 536870912 | bytes 17301504 | tf_op jit(solution)/shard_map/pallas_call | solution.py:28
  114.1 4.6 %shard_map.83.refs_0_ = f32[16,64,256]{2,1,0:T(8,128)S(1)} custom-call(bf16[16,128,128]{2,1,0:T(8,128)(2,1)S(1)} %all_to_all.20.refs_0_, bf16[4096,1024]{1,0:T(8,128)(2,1)S(1)} %get-tuple-element.62.refs_1_, bf16[4096,1024]{1,0:T(8,128)(2,1)S(1)} %get-tuple-element.63.refs_2_), custom_call_target="tpu_custom_call" | custom-call | flops 1073741824 | bytes 17301504 | tf_op jit(solution)/shard_map/pallas_call | solution.py:28
  121.5 4.2 %all-to-all-start.3 = ((bf16[16,64,256]{2,1,0:T(8,128)(2,1)}), bf16[16,64,256]{2,1,0:T(8,128)(2,1)S(1)}, u32[]{:S(2)}, u32[]{:S(2)}) async-start(bf16[16,64,256]{2,1,0:T(8,128)(2,1)} %shard_map.84.refs_4_), calls=%async_computation.3 | async-start | bytes 1048576 | tf_op jit(solution)/shard_map/all_to_all | solution.py:514
  127.5 2.0 %collective-permute-start.16 = (bf16[4,2,128,128]{3,2,1,0:T(8,128)(2,1)S(1)}, bf16[4,2,128,128]{3,2,1,0:T(8,128)(2,1)S(1)}, u32[]{:S(2)}, u32[]{:S(2)}) collective-permute-start(bf16[4,2,128,128]{3,2,1,0:T(8,128)(2,1)S(1)} %shard_map.87), channel_id=1, source_target_pairs={{0,4},{2,6},{4,0},{6,2},{8,12},{10,14},{12,8},{14,10},{16,20},{18,... | collective-permute-start | bytes 786440 | tf_op jit(solution)/shard_map/ppermute | solution.py:427
  129.4 10.0 %collective-permute-done.16.refs_2_ = bf16[4,2,128,128]{3,2,1,0:T(8,128)(2,1)S(1)} collective-permute-done((bf16[4,2,128,128]{3,2,1,0:T(8,128)(2,1)S(1)}, bf16[4,2,128,128]{3,2,1,0:T(8,128)(2,1)S(1)}, u32[]{:S(2)}, u32[]{:S(2)}) %collective-permute-start.16) | collective-permute-done | bytes 262176 | tf_op jit(solution)/shard_map/ppermute | solution.py:427
  (45 shorter events, 17.3 us)
Async XLA Ops:
  0.6 21.9 %all-to-all-start = ((bf16[16,64,256]{2,1,0:T(8,128)(2,1)}), bf16[16,64,256]{2,1,0:T(8,128)(2,1)S(1)}, u32[]{:S(2)}, u32[]{:S(2)}) async-start(bf16[16,64,256]{2,1,0:T(8,128)(2,1)} %bitcast.39), calls=%async_computation | async-start | bytes 1048576 | tf_op jit(solution)/shard_map/all_to_all | solution.py:445
  8.0 1.0 copy-start
  9.1 1.0 copy-start.1
  10.5 7.5 %collective-permute-start = (bf16[1,2,256,128]{3,2,1,0:T(8,128)(2,1)S(1)}, bf16[1,2,256,128]{3,2,1,0:T(8,128)(2,1)S(1)}, u32[]{:S(2)}, u32[]{:S(2)}) collective-permute-start(bf16[1,2,256,128]{3,2,1,0:T(8,128)(2,1)S(1)} %get-tuple-element.40), channel_id=1, source_target_pairs={{0,4},{2,6},{4,0},{6,2},{8,12},{10,14},{12,8},{14,10},{16,20},{18,... | collective-permute-start | bytes 393224 | tf_op jit(solution)/shard_map/ppermute | solution.py:427
  18.0 1.4 %collective-permute-start.1 = (bf16[2,256,128]{2,1,0:T(8,128)(2,1)S(1)}, bf16[2,256,128]{2,1,0:T(8,128)(2,1)S(1)}, u32[]{:S(2)}, u32[]{:S(2)}) collective-permute-start(bf16[2,256,128]{2,1,0:T(8,128)(2,1)S(1)} %get-tuple-element.42), channel_id=1, source_target_pairs={{0,2},{2,0},{4,6},{6,4},{8,10},{10,8},{12,14},{14,12},{16,18},{18,... | collective-permute-start | bytes 393224 | tf_op jit(solution)/shard_map/ppermute | solution.py:427
  22.5 11.1 %collective-permute-start.2 = (bf16[3,2,256,128]{3,2,1,0:T(8,128)(2,1)S(1)}, bf16[3,2,256,128]{3,2,1,0:T(8,128)(2,1)S(1)}, u32[]{:S(2)}, u32[]{:S(2)}) collective-permute-start(bf16[3,2,256,128]{3,2,1,0:T(8,128)(2,1)S(1)} %shard_map.71), channel_id=1, source_target_pairs={{0,4},{2,6},{4,0},{6,2},{8,12},{10,14},{12,8},{14,10},{16,20},{18,... | collective-permute-start | bytes 1179656 | tf_op jit(solution)/shard_map/ppermute | solution.py:427
  23.0 14.3 %collective-permute-start.7 = (bf16[16,64,256]{2,1,0:T(8,128)(2,1)S(1)}, bf16[16,64,256]{2,1,0:T(8,128)(2,1)S(1)}, u32[]{:S(2)}, u32[]{:S(2)}) collective-permute-start(bf16[16,64,256]{2,1,0:T(8,128)(2,1)S(1)} %all-to-all-done.refs_1_.m_ref), channel_id=1, source_target_pairs={{0,1},{1,0},{2,3},{3,2},{4,5},{5,4},{6,7},{7,6},{8,9},{9,8},{10,11... | collective-permute-start | bytes 1572872 | tf_op jit(solution)/shard_map/ppermute | solution.py:441
  24.5 16.8 %collective-permute-start.6 = (bf16[2,2,256,128]{3,2,1,0:T(8,128)(2,1)S(1)}, bf16[2,2,256,128]{3,2,1,0:T(8,128)(2,1)S(1)}, u32[]{:S(2)}, u32[]{:S(2)}) collective-permute-start(bf16[2,2,256,128]{3,2,1,0:T(8,128)(2,1)S(1)} %shard_map.70), channel_id=1, source_target_pairs={{0,16},{2,18},{4,20},{6,22},{8,24},{10,26},{12,28},{14,30},{16,0},... | collective-permute-start | bytes 786440 | tf_op jit(solution)/shard_map/ppermute | solution.py:427
  33.7 1.4 %collective-permute-start.3 = (bf16[2,256,128]{2,1,0:T(8,128)(2,1)S(1)}, bf16[2,256,128]{2,1,0:T(8,128)(2,1)S(1)}, u32[]{:S(2)}, u32[]{:S(2)}) collective-permute-start(bf16[2,256,128]{2,1,0:T(8,128)(2,1)S(1)} %get-tuple-element.46), channel_id=1, source_target_pairs={{0,2},{2,0},{4,6},{6,4},{8,10},{10,8},{12,14},{14,12},{16,18},{18,... | collective-permute-start | bytes 393224 | tf_op jit(solution)/shard_map/ppermute | solution.py:427
  33.8 1.5 %collective-permute-start.4 = (bf16[2,256,128]{2,1,0:T(8,128)(2,1)S(1)}, bf16[2,256,128]{2,1,0:T(8,128)(2,1)S(1)}, u32[]{:S(2)}, u32[]{:S(2)}) collective-permute-start(bf16[2,256,128]{2,1,0:T(8,128)(2,1)S(1)} %get-tuple-element.47), channel_id=1, source_target_pairs={{0,2},{2,0},{4,6},{6,4},{8,10},{10,8},{12,14},{14,12},{16,18},{18,... | collective-permute-start | bytes 393224 | tf_op jit(solution)/shard_map/ppermute | solution.py:427
  34.3 1.3 collective-permute-start.5
  41.2 18.6 %all-to-all-start.1 = ((bf16[16,128,128]{2,1,0:T(8,128)(2,1)}), bf16[16,128,128]{2,1,0:T(8,128)(2,1)S(1)}, u32[]{:S(2)}, u32[]{:S(2)}) async-start(bf16[16,128,128]{2,1,0:T(8,128)(2,1)} %shard_map.75), calls=%async_computation.1 | async-start | bytes 1048576 | tf_op jit(solution)/shard_map/all_to_all | solution.py:424
  45.1 29.3 %collective-permute-start.8 = (bf16[2,2,256,128]{3,2,1,0:T(8,128)(2,1)S(1)}, bf16[2,2,256,128]{3,2,1,0:T(8,128)(2,1)S(1)}, u32[]{:S(2)}, u32[]{:S(2)}) collective-permute-start(bf16[2,2,256,128]{3,2,1,0:T(8,128)(2,1)S(1)} %get-tuple-element.56), channel_id=1, source_target_pairs={{0,8},{2,10},{4,12},{6,14},{8,0},{10,2},{12,4},{14,6},{16,24},{18,... | collective-permute-start | bytes 786440 | tf_op jit(solution)/shard_map/ppermute | solution.py:427
  47.0 27.3 %collective-permute-start.9 = (bf16[2,2,256,128]{3,2,1,0:T(8,128)(2,1)S(1)}, bf16[2,2,256,128]{3,2,1,0:T(8,128)(2,1)S(1)}, u32[]{:S(2)}, u32[]{:S(2)}) collective-permute-start(bf16[2,2,256,128]{3,2,1,0:T(8,128)(2,1)S(1)} %get-tuple-element.57), channel_id=1, source_target_pairs={{0,24},{2,26},{4,28},{6,30},{8,16},{10,18},{12,20},{14,22},{16,8},... | collective-permute-start | bytes 786440 | tf_op jit(solution)/shard_map/ppermute | solution.py:427
  72.0 14.5 %collective-permute-start.10 = (bf16[2,2,128,128]{3,2,1,0:T(8,128)(2,1)S(1)}, bf16[2,2,128,128]{3,2,1,0:T(8,128)(2,1)S(1)}, u32[]{:S(2)}, u32[]{:S(2)}) collective-permute-start(bf16[2,2,128,128]{3,2,1,0:T(8,128)(2,1)S(1)} %bitcast.40), channel_id=1, source_target_pairs={{0,16},{2,18},{4,20},{6,22},{8,24},{10,26},{12,28},{14,30},{16,0},... | collective-permute-start | bytes 393224 | tf_op jit(solution)/shard_map/ppermute | solution.py:427
  106.6 14.1 %collective-permute-start.13 = (bf16[8,64,256]{2,1,0:T(8,128)(2,1)S(1)}, bf16[8,64,256]{2,1,0:T(8,128)(2,1)S(1)}, u32[]{:S(2)}, u32[]{:S(2)}) collective-permute-start(bf16[8,64,256]{2,1,0:T(8,128)(2,1)S(1)} %shard_map.80.refs_1_), channel_id=1, source_target_pairs={{0,1},{1,0},{2,3},{3,2},{4,5},{5,4},{6,7},{7,6},{8,9},{9,8},{10,11... | collective-permute-start | bytes 786440 | tf_op jit(solution)/shard_map/ppermute | solution.py:441
  110.6 10.1 %collective-permute-start.14 = (bf16[8,64,256]{2,1,0:T(8,128)(2,1)S(1)}, bf16[8,64,256]{2,1,0:T(8,128)(2,1)S(1)}, u32[]{:S(2)}, u32[]{:S(2)}) collective-permute-start(bf16[8,64,256]{2,1,0:T(8,128)(2,1)S(1)} %shard_map.81.refs_2_), channel_id=1, source_target_pairs={{0,1},{1,0},{2,3},{3,2},{4,5},{5,4},{6,7},{7,6},{8,9},{9,8},{10,11... | collective-permute-start | bytes 786440 | tf_op jit(solution)/shard_map/ppermute | solution.py:441
  111.2 8.2 %collective-permute-start.12 = (bf16[2,2,128,128]{3,2,1,0:T(8,128)(2,1)S(1)}, bf16[2,2,128,128]{3,2,1,0:T(8,128)(2,1)S(1)}, u32[]{:S(2)}, u32[]{:S(2)}) collective-permute-start(bf16[2,2,128,128]{3,2,1,0:T(8,128)(2,1)S(1)} %get-tuple-element.72), channel_id=1, source_target_pairs={{0,24},{2,26},{4,28},{6,30},{8,16},{10,18},{12,20},{14,22},{16,8},... | collective-permute-start | bytes 393224 | tf_op jit(solution)/shard_map/ppermute | solution.py:427
  112.7 8.0 %collective-permute-start.11 = (bf16[2,2,128,128]{3,2,1,0:T(8,128)(2,1)S(1)}, bf16[2,2,128,128]{3,2,1,0:T(8,128)(2,1)S(1)}, u32[]{:S(2)}, u32[]{:S(2)}) collective-permute-start(bf16[2,2,128,128]{3,2,1,0:T(8,128)(2,1)S(1)} %get-tuple-element.73), channel_id=1, source_target_pairs={{0,8},{2,10},{4,12},{6,14},{8,0},{10,2},{12,4},{14,6},{16,24},{18,... | collective-permute-start | bytes 393224 | tf_op jit(solution)/shard_map/ppermute | solution.py:427
  121.5 19.0 %all-to-all-start.3 = ((bf16[16,64,256]{2,1,0:T(8,128)(2,1)}), bf16[16,64,256]{2,1,0:T(8,128)(2,1)S(1)}, u32[]{:S(2)}, u32[]{:S(2)}) async-start(bf16[16,64,256]{2,1,0:T(8,128)(2,1)} %shard_map.84.refs_4_), calls=%async_computation.3 | async-start | bytes 1048576 | tf_op jit(solution)/shard_map/all_to_all | solution.py:514
  125.8 1.6 %collective-permute-start.15 = (bf16[4,2,128,128]{3,2,1,0:T(8,128)(2,1)S(1)}, bf16[4,2,128,128]{3,2,1,0:T(8,128)(2,1)S(1)}, u32[]{:S(2)}, u32[]{:S(2)}) collective-permute-start(bf16[4,2,128,128]{3,2,1,0:T(8,128)(2,1)S(1)} %get-tuple-element.66), channel_id=1, source_target_pairs={{0,2},{2,0},{4,6},{6,4},{8,10},{10,8},{12,14},{14,12},{16,18},{18,... | collective-permute-start | bytes 786440 | tf_op jit(solution)/shard_map/ppermute | solution.py:427
  127.5 12.0 %collective-permute-start.16 = (bf16[4,2,128,128]{3,2,1,0:T(8,128)(2,1)S(1)}, bf16[4,2,128,128]{3,2,1,0:T(8,128)(2,1)S(1)}, u32[]{:S(2)}, u32[]{:S(2)}) collective-permute-start(bf16[4,2,128,128]{3,2,1,0:T(8,128)(2,1)S(1)} %shard_map.87), channel_id=1, source_target_pairs={{0,4},{2,6},{4,0},{6,2},{8,12},{10,14},{12,8},{14,10},{16,20},{18,... | collective-permute-start | bytes 786440 | tf_op jit(solution)/shard_map/ppermute | solution.py:427

commit v2 on v1

--- a/solution.py
+++ b/solution.py
@@ -123,30 +123,50 @@
     return whole(kernel, out, *pieces, after=after)[0]
 
 
-def project(mem, w_key, w_value, before=None, after=()):
-    blocks, rows, depth = mem.shape
+def fetch(arrays, after=()):
+    n = len(arrays)
+
+    def kernel(*refs):
+        copies = [pltpu.make_async_copy(refs[i], refs[i - n - 1], refs[-1].at[i]) for i in range(n)]
+        for copy in copies:
+            copy.start()
+        for copy in copies:
+            copy.wait()
+
+    anywhere = pl.BlockSpec(memory_space=pl.ANY)
+    return pl.pallas_call(
+        kernel,
+        in_specs=[anywhere] * (n + len(after)),
+        out_specs=[VMEM] * n,
+        out_shape=[pltpu.VMEM(x.shape, x.dtype) for x in arrays],
+        scratch_shapes=[pltpu.SemaphoreType.DMA((n,))],
+        compiler_params=pltpu.CompilerParams(vmem_limit_bytes=12 * MIB),
+        cost_estimate=pl.CostEstimate(
+            flops=0, bytes_accessed=sum(x.size * x.dtype.itemsize for x in arrays), transcendentals=0
+        ),
+    )(*[pltpu.with_memory_space_constraint(x, pltpu.MemorySpace.HBM) for x in arrays], *after)
+
+
+def project(mems, w_key, w_value, after=()):
+    blocks, rows, depth = mems[0].shape
     depth *= blocks
     width = w_key.shape[1]
     heads = width // HD
     tile = math.gcd(width, 256)
-    ahead = 0 if before is None else before.shape[1]
-
-    def kernel(m_ref, k_ref, v_ref, *refs):
+
+    def kernel(k_ref, v_ref, *refs):
         out_ref = refs[-1]
-        if ahead:
-            out_ref[:, :ahead, :] = refs[0][...]
-        m = jnp.concatenate([m_ref[b] for b in range(blocks)], axis=1)
+        m = [jnp.concatenate([ref[b] for ref in refs[:-1]], axis=0) for b in range(blocks)]
+        m = jnp.concatenate(m, axis=1)
         for at in range(0, width, tile):
             key = dot(m, k_ref[:, at : at + tile], 1, 0).astype(BF16)
             value = dot(m, v_ref[:, at : at + tile], 1, 0).astype(BF16)
             for h in range(tile // HD):
-                out_ref[at // HD + h, ahead:, :] = jnp.concatenate(
-                    [head_of(key, h), head_of(value, h)], axis=1
-                )
-
-    out = [jax.ShapeDtypeStruct((heads, ahead + rows, 2 * HD), BF16)]
-    args = (mem, w_key, w_value) + (() if before is None else (before,))
-    return whole(kernel, out, *args, after=after, flops=4 * rows * depth * width)[0]
+                out_ref[at // HD + h] = jnp.concatenate([head_of(key, h), head_of(value, h)], axis=1)
+
+    total = rows * len(mems)
+    out = [jax.ShapeDtypeStruct((heads, total, 2 * HD), BF16)]
+    return whole(kernel, out, w_key, w_value, *mems, after=after)[0]
 
 
 def memory_grad(dkv, at, rows, w_key, w_value, blocks, dtype, span=(0, 1), after=()):
@@ -170,59 +190,6 @@
     out = [jax.ShapeDtypeStruct(((high - low) // each, rows, each), dtype)]
     flops = 4 * rows * (high - low) * width
     return whole(kernel, out, dkv, w_key, w_value, after=after, flops=flops)[0]
-
-
-def project_and_fetch(mem, w_key, w_value):
-    blocks, rows, each = mem.shape
-    depth, width = w_key.shape
-    heads = width // HD
-    steps = math.gcd(blocks, 8)
-    tall, per = depth // steps, blocks // steps
-
-    def kernel(m_ref, k_hbm, v_hbm, out_ref, k_ref, v_ref, key_ref, value_ref, sem):
-        copies = []
-        for i in range(steps):
-            here = pl.ds(i * tall, tall)
-            copies.append(
-                [
-                    pltpu.make_async_copy(k_hbm.at[here], k_ref.at[here], sem.at[0, i]),
-                    pltpu.make_async_copy(v_hbm.at[here], v_ref.at[here], sem.at[1, i]),
-                ]
-            )
-        for pair in copies:
-            for copy in pair:
-                copy.start()
-        for i, pair in enumerate(copies):
-            here = pl.ds(i * tall, tall)
-            m = jnp.concatenate([m_ref[b] for b in range(i * per, (i + 1) * per)], axis=1)
-            for copy, ref, sum_ref in zip(pair, (k_ref, v_ref), (key_ref, value_ref)):
-                copy.wait()
-                part = dot(m, ref[here, :], 1, 0)
-                sum_ref[...] = part if i == 0 else sum_ref[...] + part
-        key, value = key_ref[...].astype(BF16), value_ref[...].astype(BF16)
-        for h in range(heads):
-            out_ref[h] = jnp.concatenate([head_of(key, h), head_of(value, h)], axis=1)
-
-    anywhere = pl.BlockSpec(memory_space=pl.ANY)
-    return pl.pallas_call(
-        kernel,
-        in_specs=[VMEM, anywhere, anywhere],
-        out_specs=[VMEM] * 3,
-        out_shape=[
-            jax.ShapeDtypeStruct((heads, rows, 2 * HD), BF16),
-            pltpu.VMEM(w_key.shape, BF16),
-            pltpu.VMEM(w_value.shape, BF16),
-        ],
-        scratch_shapes=[
-            pltpu.VMEM((rows, width), F32),
-            pltpu.VMEM((rows, width), F32),
-            pltpu.SemaphoreType.DMA((2, steps)),
-        ],
-        compiler_params=pltpu.CompilerParams(vmem_limit_bytes=12 * MIB),
-        cost_estimate=pl.CostEstimate(
-            flops=4 * rows * depth * width, bytes_accessed=4 * depth * width, transcendentals=0
-        ),
-    )(mem, *[pltpu.with_memory_space_constraint(w, pltpu.MemorySpace.HBM) for w in (w_key, w_value)])
 
 
 def add_up(mine, others, after=()):
@@ -453,21 +420,18 @@
         early_qg = gather_far(early_qg, early)
         left_late = concat([left_late], after=(own,))
         left_late = swap(left_late, 2)
-        kv, *held = project_and_fetch(own, w_key, w_value)
-        kept, left = cross(kept_late, left_late, after=(kv,))
+        held = fetch([w_key, w_value], after=(own,))
+        kept, left = cross(kept_late, left_late, after=held[:1])
         late_qg = join(kept, [swap(x, 1) for x in left])
-        for by in range(1, col):
-            kv = project(shift(own, by), *held, kv, after=(late_qg[0],))
+        rest = [shift(own, by) for by in range(1, col)]
+        kv = project([own, *rest], *held, after=(late_qg[0],))
         early_qg, kv = lax.optimization_barrier((early_qg, kv))
         kv = deal(kv)
         late_qg = [gather_far(x, d) for x, d in zip(late_qg, late)]
         qg = [[late_qg[0], early_qg], late_qg[1:]]
     else:
         qg = deal(pair_heads(query, out_grad))
-        kv = project(own, w_key, w_value)
-        for by in range(1, col):
-            kv = project(shift(own, by), w_key, w_value, kv)
-        kv = deal(kv)
+        kv = deal(project([own, *[shift(own, by) for by in range(1, col)]], w_key, w_value))
         qg = [by_head(qg, groups)]
     if ranges > 1:
         kv = lax.all_gather(kv, "seq", axis=0, tiled=True, axis_index_groups=same_heads)

time: 142 us -> 141 us (level)
  transfers between devices with their start and end apart: 20 -> 20, of which waited for: 13 -> 13; matrix products, arithmetic and copies ran while one was open for 0% -> 0% of each run, Pallas kernels for 31% -> 30%
where the time goes in v2:
time: 141 us
  Pallas kernels  45.5 us (32%)
  waiting for transfers between devices  37.7 us (27%)
  starting transfers between devices  36.2 us (26%)
  blocking collectives  17.6 us (12%)
  local copies, waits for them, and re-layouts  2.91 us (2%)
    pallas_call x2, Pallas kernels, attention(): pl.pallas_call(functools.partial(attention_kernel, tile, math.gcd(src, ch...  24.2 us
    ppermute x14, waiting for transfers between devices, swap(): return lax.ppermute(x, 'seq', [(i, i ^ bits) for i in range(seq)])  22.6 us
    all_to_all x1, blocking collectives, deal(): lax.all_to_all(x, 'seq', 0, 0, tiled=True, axis_index_groups=same_range)  17.6 us
    ppermute x14, starting transfers between devices, swap(): return lax.ppermute(x, 'seq', [(i, i ^ bits) for i in range(seq)])  17.1 us
    pallas_call x18, Pallas kernels, whole(): pl.pallas_call(lambda *refs: kernel(*refs[:n], *refs[n + len(after):]), i...  15.5 us
    all_to_all x1, waiting for transfers between devices, deal(): lax.all_to_all(x, 'seq', 0, 0, tiled=True, axis_index_groups=same_range)  10.5 us
    all_to_all x1, starting transfers between devices, local(): own = lax.all_to_all(memory.reshape(seq, rows, -1), 'seq', 0, 0, tiled=True)  7.4 us
    pallas_call x1, Pallas kernels, fetch(): pl.pallas_call(kernel, in_specs=[anywhere] * (n + len(after)), out_specs=...  5.78 us
  transfers between devices with their start and end apart: 20, of which 13 were waited for; matrix products, arithmetic and copies ran while one was open for 0% of the time, Pallas kernels for 30%

profile of v2, /device:TPU:0, one launch (start us, length us, event | category | flops | bytes accessed | tf_op | source)
XLA Modules:
  0.0 140.7 jit_solution(280788691864625785)
XLA Ops:
  0.6 7.4 %all-to-all-start = ((bf16[16,64,256]{2,1,0:T(8,128)(2,1)}), bf16[16,64,256]{2,1,0:T(8,128)(2,1)S(1)}, u32[]{:S(2)}, u32[]{:S(2)}) async-start(bf16[16,64,256]{2,1,0:T(8,128)(2,1)} %bitcast.39), calls=%async_computation | async-start | bytes 1048576 | tf_op jit(solution)/shard_map/all_to_all | solution.py:412
  10.5 2.0 %collective-permute-start = (bf16[1,2,256,128]{3,2,1,0:T(8,128)(2,1)S(1)}, bf16[1,2,256,128]{3,2,1,0:T(8,128)(2,1)S(1)}, u32[]{:S(2)}, u32[]{:S(2)}) collective-permute-start(bf16[1,2,256,128]{3,2,1,0:T(8,128)(2,1)S(1)} %get-tuple-element.39), channel_id=1, source_target_pairs={{0,4},{2,6},{4,0},{6,2},{8,12},{10,14},{12,8},{14,10},{16,20},{18,... | collective-permute-start | bytes 393224 | tf_op jit(solution)/shard_map/ppermute | solution.py:394
  12.5 5.5 %collective-permute-done.refs_1_ = bf16[1,2,256,128]{3,2,1,0:T(8,128)(2,1)S(1)} collective-permute-done((bf16[1,2,256,128]{3,2,1,0:T(8,128)(2,1)S(1)}, bf16[1,2,256,128]{3,2,1,0:T(8,128)(2,1)S(1)}, u32[]{:S(2)}, u32[]{:S(2)}) %collective-permute-start) | collective-permute-done | bytes 131104 | tf_op jit(solution)/shard_map/ppermute | solution.py:394
  19.5 3.0 %all-to-all-done.refs_1_.refs_2_ = bf16[16,64,256]{2,1,0:T(8,128)(2,1)S(1)} async-done(((bf16[16,64,256]{2,1,0:T(8,128)(2,1)}), bf16[16,64,256]{2,1,0:T(8,128)(2,1)S(1)}, u32[]{:S(2)}, u32[]{:S(2)}) %all-to-all-start) | async-done | bytes 524320 | tf_op jit(solution)/shard_map/all_to_all | solution.py:412
  23.0 1.5 %collective-permute-start.7 = (bf16[16,64,256]{2,1,0:T(8,128)(2,1)S(1)}, bf16[16,64,256]{2,1,0:T(8,128)(2,1)S(1)}, u32[]{:S(2)}, u32[]{:S(2)}) collective-permute-start(bf16[16,64,256]{2,1,0:T(8,128)(2,1)S(1)} %all-to-all-done.refs_1_.refs_2_), channel_id=1, source_target_pairs={{0,1},{1,0},{2,3},{3,2},{4,5},{5,4},{6,7},{7,6},{8,9},{9,8},{10,11... | collective-permute-start | bytes 1572872 | tf_op jit(solution)/shard_map/ppermute | solution.py:408
  24.5 1.9 %collective-permute-start.6 = (bf16[2,2,256,128]{3,2,1,0:T(8,128)(2,1)S(1)}, bf16[2,2,256,128]{3,2,1,0:T(8,128)(2,1)S(1)}, u32[]{:S(2)}, u32[]{:S(2)}) collective-permute-start(bf16[2,2,256,128]{3,2,1,0:T(8,128)(2,1)S(1)} %shard_map.70), channel_id=1, source_target_pairs={{0,16},{2,18},{4,20},{6,22},{8,24},{10,26},{12,28},{14,30},{16,0},... | collective-permute-start | bytes 786440 | tf_op jit(solution)/shard_map/ppermute | solution.py:394
  26.4 5.8 %shard_map.72 = (bf16[4096,1024]{1,0:T(8,128)(2,1)S(1)}, bf16[4096,1024]{1,0:T(8,128)(2,1)S(1)}) custom-call(bf16[4096,1024]{1,0:T(8,128)(2,1)} %refs_1_.5, bf16[4096,1024]{1,0:T(8,128)(2,1)} %refs_2_.3, bf16[16,64,256]{2,1,0:T(8,128)(2,1)S(1)} %all-to-all-done.refs_1_.refs_2_), custom_call_target="tpu_custom_call" | custom-call | bytes 16777216 | tf_op jit(solution)/shard_map/pallas_call | solution.py:137
  35.7 1.6 %collective-permute-done.7.refs_3_ = bf16[16,64,256]{2,1,0:T(8,128)(2,1)S(1)} collective-permute-done((bf16[16,64,256]{2,1,0:T(8,128)(2,1)S(1)}, bf16[16,64,256]{2,1,0:T(8,128)(2,1)S(1)}, u32[]{:S(2)}, u32[]{:S(2)}) %collective-permute-start.7) | collective-permute-done | bytes 524320 | tf_op jit(solution)/shard_map/ppermute | solution.py:408
  37.3 3.3 %shard_map.75 = bf16[16,128,128]{2,1,0:T(8,128)(2,1)} custom-call(bf16[4096,1024]{1,0:T(8,128)(2,1)S(1)} %get-tuple-element.43.refs_2_.refs_0_, bf16[4096,1024]{1,0:T(8,128)(2,1)S(1)} %get-tuple-element.50.refs_1_, bf16[16,64,256]{2,1,0:T(8,128)(2,1)S(1)} %all-to-all-done.refs_1_.refs_2_, bf16[16,64,256]{2,1,0:T(8,128)(2,1)S(1)} %collective-permute-done.7.refs_3_, ...), custom_call_target="tpu_custom_call" | custom-call | bytes 17825792 | tf_op jit(solution)/shard_map/pallas_call | solution.py:28
  40.6 3.8 %all-to-all-start.1 = ((bf16[16,128,128]{2,1,0:T(8,128)(2,1)}), bf16[16,128,128]{2,1,0:T(8,128)(2,1)S(1)}, u32[]{:S(2)}, u32[]{:S(2)}) async-start(bf16[16,128,128]{2,1,0:T(8,128)(2,1)} %shard_map.75), calls=%async_computation.1 | async-start | bytes 1048576 | tf_op jit(solution)/shard_map/all_to_all | solution.py:391
  44.4 2.0 %collective-permute-start.8 = (bf16[2,2,256,128]{3,2,1,0:T(8,128)(2,1)S(1)}, bf16[2,2,256,128]{3,2,1,0:T(8,128)(2,1)S(1)}, u32[]{:S(2)}, u32[]{:S(2)}) collective-permute-start(bf16[2,2,256,128]{3,2,1,0:T(8,128)(2,1)S(1)} %get-tuple-element.54), channel_id=1, source_target_pairs={{0,8},{2,10},{4,12},{6,14},{8,0},{10,2},{12,4},{14,6},{16,24},{18,... | collective-permute-start | bytes 786440 | tf_op jit(solution)/shard_map/ppermute | solution.py:394
  46.4 2.4 %collective-permute-start.9 = (bf16[2,2,256,128]{3,2,1,0:T(8,128)(2,1)S(1)}, bf16[2,2,256,128]{3,2,1,0:T(8,128)(2,1)S(1)}, u32[]{:S(2)}, u32[]{:S(2)}) collective-permute-start(bf16[2,2,256,128]{3,2,1,0:T(8,128)(2,1)S(1)} %get-tuple-element.55), channel_id=1, source_target_pairs={{0,24},{2,26},{4,28},{6,30},{8,16},{10,18},{12,20},{14,22},{16,8},... | collective-permute-start | bytes 786440 | tf_op jit(solution)/shard_map/ppermute | solution.py:394
  48.8 10.5 %all-to-all-done.1 = bf16[16,128,128]{2,1,0:T(8,128)(2,1)S(1)} async-done(((bf16[16,128,128]{2,1,0:T(8,128)(2,1)}), bf16[16,128,128]{2,1,0:T(8,128)(2,1)S(1)}, u32[]{:S(2)}, u32[]{:S(2)}) %all-to-all-start.1) | async-done | bytes 524320 | tf_op jit(solution)/shard_map/all_to_all | solution.py:391
  59.3 12.1 %shard_map.77 = (bf16[1,1024,128]{2,1,0:T(8,128)(2,1)S(1)}, f32[1,2048,128]{2,1,0:T(8,128)S(1)}) custom-call(bf16[1,2048,128]{2,1,0:T(8,128)(2,1)S(1)} %bitcast.28, bf16[1,2048,128]{2,1,0:T(8,128)(2,1)S(1)} %bitcast.25), custom_call_target="tpu_custom_call" | custom-call | flops 10737418240 | bytes 4194304 | tf_op jit(solution)/shard_map/pallas_call | solution.py:349
  71.4 2.3 %collective-permute-start.10 = (bf16[2,2,128,128]{3,2,1,0:T(8,128)(2,1)S(1)}, bf16[2,2,128,128]{3,2,1,0:T(8,128)(2,1)S(1)}, u32[]{:S(2)}, u32[]{:S(2)}) collective-permute-start(bf16[2,2,128,128]{3,2,1,0:T(8,128)(2,1)S(1)} %bitcast.40), channel_id=1, source_target_pairs={{0,16},{2,18},{4,20},{6,22},{8,24},{10,26},{12,28},{14,30},{16,0},... | collective-permute-start | bytes 393224 | tf_op jit(solution)/shard_map/ppermute | solution.py:394
  73.8 12.1 %shard_map.79 = (bf16[1,1024,128]{2,1,0:T(8,128)(2,1)S(1)}, bf16[1,2048,128]{2,1,0:T(8,128)(2,1)S(1)}, bf16[4096,1024]{1,0:T(8,128)(2,1)S(1)}, bf16[4096,1024]{1,0:T(8,128)(2,1)S(1)}) custom-call(bf16[1,2048,128]{2,1,0:T(8,128)(2,1)S(1)} %bitcast.29, bf16[1,2048,128]{2,1,0:T(8,128)(2,1)S(1)} %bitcast.26, ...), custom_call_target="tpu_custom_call" | custom-call | flops 10737418240 | bytes 4194304 | tf_op jit(solution)/shard_map/pallas_call | solution.py:349
  85.9 17.6 %all_to_all.20.refs_0_ = bf16[16,128,128]{2,1,0:T(8,128)(2,1)S(1)} all-to-all(bf16[16,128,128]{2,1,0:T(8,128)(2,1)S(1)} %bitcast.27), channel_id=1, replica_groups={{0,2,4,6,8,10,12,14,16,18,20,22,24,26,28,30},{1,3,5,7,9,11,13,15,17,19,..., dimensions={0} | all-to-all | bytes 1048576 | tf_op jit(solution)/shard_map/all_to_all | solution.py:391
  103.5 2.5 %shard_map.80.refs_1_ = bf16[8,64,256]{2,1,0:T(8,128)(2,1)S(1)} custom-call(bf16[16,128,128]{2,1,0:T(8,128)(2,1)S(1)} %all_to_all.20.refs_0_, bf16[4096,1024]{1,0:T(8,128)(2,1)S(1)} %get-tuple-element.60.refs_1_, bf16[4096,1024]{1,0:T(8,128)(2,1)S(1)} %get-tuple-element.61.refs_2_), custom_call_target="tpu_custom_call" | custom-call | flops 536870912 | bytes 17301504 | tf_op jit(solution)/shard_map/pallas_call | solution.py:28
  106.0 1.6 %collective-permute-start.13 = (bf16[8,64,256]{2,1,0:T(8,128)(2,1)S(1)}, bf16[8,64,256]{2,1,0:T(8,128)(2,1)S(1)}, u32[]{:S(2)}, u32[]{:S(2)}) collective-permute-start(bf16[8,64,256]{2,1,0:T(8,128)(2,1)S(1)} %shard_map.80.refs_1_), channel_id=1, source_target_pairs={{0,1},{1,0},{2,3},{3,2},{4,5},{5,4},{6,7},{7,6},{8,9},{9,8},{10,11... | collective-permute-start | bytes 786440 | tf_op jit(solution)/shard_map/ppermute | solution.py:408
  107.5 2.5 %shard_map.81.refs_2_ = bf16[8,64,256]{2,1,0:T(8,128)(2,1)S(1)} custom-call(bf16[16,128,128]{2,1,0:T(8,128)(2,1)S(1)} %all_to_all.20.refs_0_, bf16[4096,1024]{1,0:T(8,128)(2,1)S(1)} %get-tuple-element.60.refs_1_, bf16[4096,1024]{1,0:T(8,128)(2,1)S(1)} %get-tuple-element.61.refs_2_), custom_call_target="tpu_custom_call" | custom-call | flops 536870912 | bytes 17301504 | tf_op jit(solution)/shard_map/pallas_call | solution.py:28
  113.5 4.6 %shard_map.83.refs_0_ = f32[16,64,256]{2,1,0:T(8,128)S(1)} custom-call(bf16[16,128,128]{2,1,0:T(8,128)(2,1)S(1)} %all_to_all.20.refs_0_, bf16[4096,1024]{1,0:T(8,128)(2,1)S(1)} %get-tuple-element.60.refs_1_, bf16[4096,1024]{1,0:T(8,128)(2,1)S(1)} %get-tuple-element.61.refs_2_), custom_call_target="tpu_custom_call" | custom-call | flops 1073741824 | bytes 17301504 | tf_op jit(solution)/shard_map/pallas_call | solution.py:28
  120.9 4.2 %all-to-all-start.3 = ((bf16[16,64,256]{2,1,0:T(8,128)(2,1)}), bf16[16,64,256]{2,1,0:T(8,128)(2,1)S(1)}, u32[]{:S(2)}, u32[]{:S(2)}) async-start(bf16[16,64,256]{2,1,0:T(8,128)(2,1)} %shard_map.84.refs_4_), calls=%async_computation.3 | async-start | bytes 1048576 | tf_op jit(solution)/shard_map/all_to_all | solution.py:478
  126.9 2.0 %collective-permute-start.16 = (bf16[4,2,128,128]{3,2,1,0:T(8,128)(2,1)S(1)}, bf16[4,2,128,128]{3,2,1,0:T(8,128)(2,1)S(1)}, u32[]{:S(2)}, u32[]{:S(2)}) collective-permute-start(bf16[4,2,128,128]{3,2,1,0:T(8,128)(2,1)S(1)} %shard_map.87), channel_id=1, source_target_pairs={{0,4},{2,6},{4,0},{6,2},{8,12},{10,14},{12,8},{14,10},{16,20},{18,... | collective-permute-start | bytes 786440 | tf_op jit(solution)/shard_map/ppermute | solution.py:394
  128.8 10.0 %collective-permute-done.16.refs_2_ = bf16[4,2,128,128]{3,2,1,0:T(8,128)(2,1)S(1)} collective-permute-done((bf16[4,2,128,128]{3,2,1,0:T(8,128)(2,1)S(1)}, bf16[4,2,128,128]{3,2,1,0:T(8,128)(2,1)S(1)}, u32[]{:S(2)}, u32[]{:S(2)}) %collective-permute-start.16) | collective-permute-done | bytes 262176 | tf_op jit(solution)/shard_map/ppermute | solution.py:394
  (45 shorter events, 17.8 us)
Async XLA Ops:
  0.6 21.9 %all-to-all-start = ((bf16[16,64,256]{2,1,0:T(8,128)(2,1)}), bf16[16,64,256]{2,1,0:T(8,128)(2,1)S(1)}, u32[]{:S(2)}, u32[]{:S(2)}) async-start(bf16[16,64,256]{2,1,0:T(8,128)(2,1)} %bitcast.39), calls=%async_computation | async-start | bytes 1048576 | tf_op jit(solution)/shard_map/all_to_all | solution.py:412
  8.0 1.0 copy-start
  9.1 1.0 copy-start.1
  10.5 7.5 %collective-permute-start = (bf16[1,2,256,128]{3,2,1,0:T(8,128)(2,1)S(1)}, bf16[1,2,256,128]{3,2,1,0:T(8,128)(2,1)S(1)}, u32[]{:S(2)}, u32[]{:S(2)}) collective-permute-start(bf16[1,2,256,128]{3,2,1,0:T(8,128)(2,1)S(1)} %get-tuple-element.39), channel_id=1, source_target_pairs={{0,4},{2,6},{4,0},{6,2},{8,12},{10,14},{12,8},{14,10},{16,20},{18,... | collective-permute-start | bytes 393224 | tf_op jit(solution)/shard_map/ppermute | solution.py:394
  18.0 1.4 %collective-permute-start.1 = (bf16[2,256,128]{2,1,0:T(8,128)(2,1)S(1)}, bf16[2,256,128]{2,1,0:T(8,128)(2,1)S(1)}, u32[]{:S(2)}, u32[]{:S(2)}) collective-permute-start(bf16[2,256,128]{2,1,0:T(8,128)(2,1)S(1)} %get-tuple-element.41), channel_id=1, source_target_pairs={{0,2},{2,0},{4,6},{6,4},{8,10},{10,8},{12,14},{14,12},{16,18},{18,... | collective-permute-start | bytes 393224 | tf_op jit(solution)/shard_map/ppermute | solution.py:394
  22.5 11.1 %collective-permute-start.2 = (bf16[3,2,256,128]{3,2,1,0:T(8,128)(2,1)S(1)}, bf16[3,2,256,128]{3,2,1,0:T(8,128)(2,1)S(1)}, u32[]{:S(2)}, u32[]{:S(2)}) collective-permute-start(bf16[3,2,256,128]{3,2,1,0:T(8,128)(2,1)S(1)} %shard_map.71), channel_id=1, source_target_pairs={{0,4},{2,6},{4,0},{6,2},{8,12},{10,14},{12,8},{14,10},{16,20},{18,... | collective-permute-start | bytes 1179656 | tf_op jit(solution)/shard_map/ppermute | solution.py:394
  23.0 14.3 %collective-permute-start.7 = (bf16[16,64,256]{2,1,0:T(8,128)(2,1)S(1)}, bf16[16,64,256]{2,1,0:T(8,128)(2,1)S(1)}, u32[]{:S(2)}, u32[]{:S(2)}) collective-permute-start(bf16[16,64,256]{2,1,0:T(8,128)(2,1)S(1)} %all-to-all-done.refs_1_.refs_2_), channel_id=1, source_target_pairs={{0,1},{1,0},{2,3},{3,2},{4,5},{5,4},{6,7},{7,6},{8,9},{9,8},{10,11... | collective-permute-start | bytes 1572872 | tf_op jit(solution)/shard_map/ppermute | solution.py:408
  24.5 16.1 %collective-permute-start.6 = (bf16[2,2,256,128]{3,2,1,0:T(8,128)(2,1)S(1)}, bf16[2,2,256,128]{3,2,1,0:T(8,128)(2,1)S(1)}, u32[]{:S(2)}, u32[]{:S(2)}) collective-permute-start(bf16[2,2,256,128]{3,2,1,0:T(8,128)(2,1)S(1)} %shard_map.70), channel_id=1, source_target_pairs={{0,16},{2,18},{4,20},{6,22},{8,24},{10,26},{12,28},{14,30},{16,0},... | collective-permute-start | bytes 786440 | tf_op jit(solution)/shard_map/ppermute | solution.py:394
  33.7 1.4 %collective-permute-start.3 = (bf16[2,256,128]{2,1,0:T(8,128)(2,1)S(1)}, bf16[2,256,128]{2,1,0:T(8,128)(2,1)S(1)}, u32[]{:S(2)}, u32[]{:S(2)}) collective-permute-start(bf16[2,256,128]{2,1,0:T(8,128)(2,1)S(1)} %get-tuple-element.45), channel_id=1, source_target_pairs={{0,2},{2,0},{4,6},{6,4},{8,10},{10,8},{12,14},{14,12},{16,18},{18,... | collective-permute-start | bytes 393224 | tf_op jit(solution)/shard_map/ppermute | solution.py:394
  33.8 1.5 %collective-permute-start.4 = (bf16[2,256,128]{2,1,0:T(8,128)(2,1)S(1)}, bf16[2,256,128]{2,1,0:T(8,128)(2,1)S(1)}, u32[]{:S(2)}, u32[]{:S(2)}) collective-permute-start(bf16[2,256,128]{2,1,0:T(8,128)(2,1)S(1)} %get-tuple-element.46), channel_id=1, source_target_pairs={{0,2},{2,0},{4,6},{6,4},{8,10},{10,8},{12,14},{14,12},{16,18},{18,... | collective-permute-start | bytes 393224 | tf_op jit(solution)/shard_map/ppermute | solution.py:394
  34.3 1.3 collective-permute-start.5
  40.6 18.6 %all-to-all-start.1 = ((bf16[16,128,128]{2,1,0:T(8,128)(2,1)}), bf16[16,128,128]{2,1,0:T(8,128)(2,1)S(1)}, u32[]{:S(2)}, u32[]{:S(2)}) async-start(bf16[16,128,128]{2,1,0:T(8,128)(2,1)} %shard_map.75), calls=%async_computation.1 | async-start | bytes 1048576 | tf_op jit(solution)/shard_map/all_to_all | solution.py:391
  44.4 29.3 %collective-permute-start.8 = (bf16[2,2,256,128]{3,2,1,0:T(8,128)(2,1)S(1)}, bf16[2,2,256,128]{3,2,1,0:T(8,128)(2,1)S(1)}, u32[]{:S(2)}, u32[]{:S(2)}) collective-permute-start(bf16[2,2,256,128]{3,2,1,0:T(8,128)(2,1)S(1)} %get-tuple-element.54), channel_id=1, source_target_pairs={{0,8},{2,10},{4,12},{6,14},{8,0},{10,2},{12,4},{14,6},{16,24},{18,... | collective-permute-start | bytes 786440 | tf_op jit(solution)/shard_map/ppermute | solution.py:394
  46.4 27.3 %collective-permute-start.9 = (bf16[2,2,256,128]{3,2,1,0:T(8,128)(2,1)S(1)}, bf16[2,2,256,128]{3,2,1,0:T(8,128)(2,1)S(1)}, u32[]{:S(2)}, u32[]{:S(2)}) collective-permute-start(bf16[2,2,256,128]{3,2,1,0:T(8,128)(2,1)S(1)} %get-tuple-element.55), channel_id=1, source_target_pairs={{0,24},{2,26},{4,28},{6,30},{8,16},{10,18},{12,20},{14,22},{16,8},... | collective-permute-start | bytes 786440 | tf_op jit(solution)/shard_map/ppermute | solution.py:394
  71.4 14.5 %collective-permute-start.10 = (bf16[2,2,128,128]{3,2,1,0:T(8,128)(2,1)S(1)}, bf16[2,2,128,128]{3,2,1,0:T(8,128)(2,1)S(1)}, u32[]{:S(2)}, u32[]{:S(2)}) collective-permute-start(bf16[2,2,128,128]{3,2,1,0:T(8,128)(2,1)S(1)} %bitcast.40), channel_id=1, source_target_pairs={{0,16},{2,18},{4,20},{6,22},{8,24},{10,26},{12,28},{14,30},{16,0},... | collective-permute-start | bytes 393224 | tf_op jit(solution)/shard_map/ppermute | solution.py:394
  106.0 14.1 %collective-permute-start.13 = (bf16[8,64,256]{2,1,0:T(8,128)(2,1)S(1)}, bf16[8,64,256]{2,1,0:T(8,128)(2,1)S(1)}, u32[]{:S(2)}, u32[]{:S(2)}) collective-permute-start(bf16[8,64,256]{2,1,0:T(8,128)(2,1)S(1)} %shard_map.80.refs_1_), channel_id=1, source_target_pairs={{0,1},{1,0},{2,3},{3,2},{4,5},{5,4},{6,7},{7,6},{8,9},{9,8},{10,11... | collective-permute-start | bytes 786440 | tf_op jit(solution)/shard_map/ppermute | solution.py:408
  110.0 10.1 %collective-permute-start.14 = (bf16[8,64,256]{2,1,0:T(8,128)(2,1)S(1)}, bf16[8,64,256]{2,1,0:T(8,128)(2,1)S(1)}, u32[]{:S(2)}, u32[]{:S(2)}) collective-permute-start(bf16[8,64,256]{2,1,0:T(8,128)(2,1)S(1)} %shard_map.81.refs_2_), channel_id=1, source_target_pairs={{0,1},{1,0},{2,3},{3,2},{4,5},{5,4},{6,7},{7,6},{8,9},{9,8},{10,11... | collective-permute-start | bytes 786440 | tf_op jit(solution)/shard_map/ppermute | solution.py:408
  110.6 8.2 %collective-permute-start.12 = (bf16[2,2,128,128]{3,2,1,0:T(8,128)(2,1)S(1)}, bf16[2,2,128,128]{3,2,1,0:T(8,128)(2,1)S(1)}, u32[]{:S(2)}, u32[]{:S(2)}) collective-permute-start(bf16[2,2,128,128]{3,2,1,0:T(8,128)(2,1)S(1)} %get-tuple-element.70), channel_id=1, source_target_pairs={{0,24},{2,26},{4,28},{6,30},{8,16},{10,18},{12,20},{14,22},{16,8},... | collective-permute-start | bytes 393224 | tf_op jit(solution)/shard_map/ppermute | solution.py:394
  112.1 8.0 %collective-permute-start.11 = (bf16[2,2,128,128]{3,2,1,0:T(8,128)(2,1)S(1)}, bf16[2,2,128,128]{3,2,1,0:T(8,128)(2,1)S(1)}, u32[]{:S(2)}, u32[]{:S(2)}) collective-permute-start(bf16[2,2,128,128]{3,2,1,0:T(8,128)(2,1)S(1)} %get-tuple-element.71), channel_id=1, source_target_pairs={{0,8},{2,10},{4,12},{6,14},{8,0},{10,2},{12,4},{14,6},{16,24},{18,... | collective-permute-start | bytes 393224 | tf_op jit(solution)/shard_map/ppermute | solution.py:394
  120.9 19.0 %all-to-all-start.3 = ((bf16[16,64,256]{2,1,0:T(8,128)(2,1)}), bf16[16,64,256]{2,1,0:T(8,128)(2,1)S(1)}, u32[]{:S(2)}, u32[]{:S(2)}) async-start(bf16[16,64,256]{2,1,0:T(8,128)(2,1)} %shard_map.84.refs_4_), calls=%async_computation.3 | async-start | bytes 1048576 | tf_op jit(solution)/shard_map/all_to_all | solution.py:478
  125.2 1.6 %collective-permute-start.15 = (bf16[4,2,128,128]{3,2,1,0:T(8,128)(2,1)S(1)}, bf16[4,2,128,128]{3,2,1,0:T(8,128)(2,1)S(1)}, u32[]{:S(2)}, u32[]{:S(2)}) collective-permute-start(bf16[4,2,128,128]{3,2,1,0:T(8,128)(2,1)S(1)} %get-tuple-element.64), channel_id=1, source_target_pairs={{0,2},{2,0},{4,6},{6,4},{8,10},{10,8},{12,14},{14,12},{16,18},{18,... | collective-permute-start | bytes 786440 | tf_op jit(solution)/shard_map/ppermute | solution.py:394
  126.9 12.0 %collective-permute-start.16 = (bf16[4,2,128,128]{3,2,1,0:T(8,128)(2,1)S(1)}, bf16[4,2,128,128]{3,2,1,0:T(8,128)(2,1)S(1)}, u32[]{:S(2)}, u32[]{:S(2)}) collective-permute-start(bf16[4,2,128,128]{3,2,1,0:T(8,128)(2,1)S(1)} %shard_map.87), channel_id=1, source_target_pairs={{0,4},{2,6},{4,0},{6,2},{8,12},{10,14},{12,8},{14,10},{16,20},{18,... | collective-permute-start | bytes 786440 | tf_op jit(solution)/shard_map/ppermute | solution.py:394

commit v3 on v2

--- a/solution.py
+++ b/solution.py
@@ -167,6 +167,40 @@
     total = rows * len(mems)
     out = [jax.ShapeDtypeStruct((heads, total, 2 * HD), BF16)]
     return whole(kernel, out, w_key, w_value, *mems, after=after)[0]
+
+
+def project_half(own, rest, w_key, w_value, low, before=(), after=()):
+    blocks, rows, each = own.shape
+    blocks //= 2
+    width = w_key.shape[1]
+    heads = width // HD
+    tile = math.gcd(width, 256)
+    total = rows * (1 + len(rest))
+    here = pl.ds(low * each, blocks * each)
+
+    def kernel(k_ref, v_ref, own_ref, *refs):
+        rest_refs, refs = refs[: len(rest)], refs[len(rest) :]
+        m = [
+            jnp.concatenate([own_ref[low + b], *[ref[b] for ref in rest_refs]], axis=0) for b in range(blocks)
+        ]
+        m = jnp.concatenate(m, axis=1)
+        for at in range(0, width, tile):
+            cols = slice(at, at + tile)
+            key = dot(m, k_ref[here, cols], 1, 0)
+            value = dot(m, v_ref[here, cols], 1, 0)
+            if not before:
+                refs[0][:, cols] = key
+                refs[1][:, cols] = value
+                continue
+            key = (key + refs[0][:, cols]).astype(BF16)
+            value = (value + refs[1][:, cols]).astype(BF16)
+            for h in range(tile // HD):
+                refs[2][at // HD + h] = jnp.concatenate([head_of(key, h), head_of(value, h)], axis=1)
+
+    out = [jax.ShapeDtypeStruct((total, width), F32)] * 2
+    if before:
+        out = [jax.ShapeDtypeStruct((heads, total, 2 * HD), BF16)]
+    return whole(kernel, out, w_key, w_value, own, *rest, *before, after=after)
 
 
 def memory_grad(dkv, at, rows, w_key, w_value, blocks, dtype, span=(0, 1), after=()):
@@ -423,8 +457,10 @@
         held = fetch([w_key, w_value], after=(own,))
         kept, left = cross(kept_late, left_late, after=held[:1])
         late_qg = join(kept, [swap(x, 1) for x in left])
-        rest = [shift(own, by) for by in range(1, col)]
-        kv = project([own, *rest], *held, after=(late_qg[0],))
+        half = seq // 2
+        rest = [[shift(x, by) for by in range(1, col)] for x in (own[:half], own[half:])]
+        sums = project_half(own, rest[0], *held, 0)
+        kv = project_half(own, rest[1], *held, half, sums, after=(late_qg[0],))[0]
         early_qg, kv = lax.optimization_barrier((early_qg, kv))
         kv = deal(kv)
         late_qg = [gather_far(x, d) for x, d in zip(late_qg, late)]

time: 141 us -> 140 us (level)
  waiting for transfers between devices: 37.7 us -> 36.1 us
    ppermute x14, waiting for transfers between devices: 22.6 us -> 20.9 us  [swap(): return lax.ppermute(x, 'seq', [(i, i ^ bits) for i in range(seq)])]
    ppermute x3 -> x4, starting transfers between devices: 3.65 us -> 4.25 us  [shift(): return lax.ppermute(x, 'col', [(i, (i + by) % col) for i in range(col)])]
    pallas_call x18 -> x19, Pallas kernels: 15.5 us -> 15.7 us  [whole(): pl.pallas_call(lambda *refs: kernel(*refs[:n], *refs[n + len(after):]), i...]
  transfers between devices with their start and end apart: 20 -> 21, of which waited for: 13 -> 11; matrix products, arithmetic and copies ran while one was open for 0% -> 0% of each run, Pallas kernels for 30% -> 30%
where the time goes in v3:
time: 140 us
  Pallas kernels  45.7 us (33%)
  starting transfers between devices  36.5 us (26%)
  waiting for transfers between devices  36.1 us (26%)
  blocking collectives  17.6 us (13%)
  local copies, waits for them, and re-layouts  2.95 us (2%)
    pallas_call x2, Pallas kernels, attention(): pl.pallas_call(functools.partial(attention_kernel, tile, math.gcd(src, ch...  24.2 us
    ppermute x14, waiting for transfers between devices, swap(): return lax.ppermute(x, 'seq', [(i, i ^ bits) for i in range(seq)])  20.9 us
    all_to_all x1, blocking collectives, deal(): lax.all_to_all(x, 'seq', 0, 0, tiled=True, axis_index_groups=same_range)  17.6 us
    ppermute x14, starting transfers between devices, swap(): return lax.ppermute(x, 'seq', [(i, i ^ bits) for i in range(seq)])  16.9 us
    pallas_call x19, Pallas kernels, whole(): pl.pallas_call(lambda *refs: kernel(*refs[:n], *refs[n + len(after):]), i...  15.7 us
    all_to_all x1, waiting for transfers between devices, deal(): lax.all_to_all(x, 'seq', 0, 0, tiled=True, axis_index_groups=same_range)  10.5 us
    all_to_all x1, starting transfers between devices, local(): own = lax.all_to_all(memory.reshape(seq, rows, -1), 'seq', 0, 0, tiled=True)  7.4 us
    pallas_call x1, Pallas kernels, fetch(): pl.pallas_call(kernel, in_specs=[anywhere] * (n + len(after)), out_specs=...  5.78 us
  transfers between devices with their start and end apart: 21, of which 11 were waited for; matrix products, arithmetic and copies ran while one was open for 0% of the time, Pallas kernels for 30%

profile of v3, /device:TPU:0, one launch (start us, length us, event | category | flops | bytes accessed | tf_op | source)
XLA Modules:
  0.0 139.7 jit_solution(909541350309010527)
XLA Ops:
  0.6 7.4 %all-to-all-start = ((bf16[16,64,256]{2,1,0:T(8,128)(2,1)}), bf16[16,64,256]{2,1,0:T(8,128)(2,1)S(1)}, u32[]{:S(2)}, u32[]{:S(2)}) async-start(bf16[16,64,256]{2,1,0:T(8,128)(2,1)} %bitcast.39), calls=%async_computation | async-start | bytes 1048576 | tf_op jit(solution)/shard_map/all_to_all | solution.py:446
  10.5 2.0 %collective-permute-start = (bf16[1,2,256,128]{3,2,1,0:T(8,128)(2,1)S(1)}, bf16[1,2,256,128]{3,2,1,0:T(8,128)(2,1)S(1)}, u32[]{:S(2)}, u32[]{:S(2)}) collective-permute-start(bf16[1,2,256,128]{3,2,1,0:T(8,128)(2,1)S(1)} %get-tuple-element.41), channel_id=1, source_target_pairs={{0,4},{2,6},{4,0},{6,2},{8,12},{10,14},{12,8},{14,10},{16,20},{18,... | collective-permute-start | bytes 393224 | tf_op jit(solution)/shard_map/ppermute | solution.py:428
  12.5 5.5 %collective-permute-done.refs_1_ = bf16[1,2,256,128]{3,2,1,0:T(8,128)(2,1)S(1)} collective-permute-done((bf16[1,2,256,128]{3,2,1,0:T(8,128)(2,1)S(1)}, bf16[1,2,256,128]{3,2,1,0:T(8,128)(2,1)S(1)}, u32[]{:S(2)}, u32[]{:S(2)}) %collective-permute-start) | collective-permute-done | bytes 131104 | tf_op jit(solution)/shard_map/ppermute | solution.py:428
  19.5 3.0 %all-to-all-done.refs_1_.refs_2_ = bf16[16,64,256]{2,1,0:T(8,128)(2,1)S(1)} async-done(((bf16[16,64,256]{2,1,0:T(8,128)(2,1)}), bf16[16,64,256]{2,1,0:T(8,128)(2,1)S(1)}, u32[]{:S(2)}, u32[]{:S(2)}) %all-to-all-start) | async-done | bytes 524320 | tf_op jit(solution)/shard_map/all_to_all | solution.py:446
  23.0 1.6 %collective-permute-start.8 = (bf16[8,64,256]{2,1,0:T(8,128)(2,1)S(1)}, bf16[8,64,256]{2,1,0:T(8,128)(2,1)S(1)}, u32[]{:S(2)}, u32[]{:S(2)}) collective-permute-start(bf16[8,64,256]{2,1,0:T(8,128)(2,1)S(1)} %get-tuple-element.74), channel_id=1, source_target_pairs={{0,1},{1,0},{2,3},{3,2},{4,5},{5,4},{6,7},{7,6},{8,9},{9,8},{10,11... | collective-permute-start | bytes 786440 | tf_op jit(solution)/shard_map/ppermute | solution.py:442
  25.1 1.9 %collective-permute-start.6 = (bf16[2,2,256,128]{3,2,1,0:T(8,128)(2,1)S(1)}, bf16[2,2,256,128]{3,2,1,0:T(8,128)(2,1)S(1)}, u32[]{:S(2)}, u32[]{:S(2)}) collective-permute-start(bf16[2,2,256,128]{3,2,1,0:T(8,128)(2,1)S(1)} %shard_map.70), channel_id=1, source_target_pairs={{0,16},{2,18},{4,20},{6,22},{8,24},{10,26},{12,28},{14,30},{16,0},... | collective-permute-start | bytes 786440 | tf_op jit(solution)/shard_map/ppermute | solution.py:428
  27.0 5.8 %shard_map.72 = (bf16[4096,1024]{1,0:T(8,128)(2,1)S(1)}, bf16[4096,1024]{1,0:T(8,128)(2,1)S(1)}) custom-call(bf16[4096,1024]{1,0:T(8,128)(2,1)} %refs_1_.5, bf16[4096,1024]{1,0:T(8,128)(2,1)} %refs_2_.3, bf16[16,64,256]{2,1,0:T(8,128)(2,1)S(1)} %all-to-all-done.refs_1_.refs_2_), custom_call_target="tpu_custom_call" | custom-call | bytes 16777216 | tf_op jit(solution)/shard_map/pallas_call | solution.py:137
  35.7 1.7 %collective-permute-done.7.refs_3_ = bf16[8,64,256]{2,1,0:T(8,128)(2,1)S(1)} collective-permute-done((bf16[8,64,256]{2,1,0:T(8,128)(2,1)S(1)}, bf16[8,64,256]{2,1,0:T(8,128)(2,1)S(1)}, u32[]{:S(2)}, u32[]{:S(2)}) %collective-permute-start.7) | collective-permute-done | bytes 262176 | tf_op jit(solution)/shard_map/ppermute | solution.py:442
  37.4 2.2 %shard_map.76 = bf16[16,128,128]{2,1,0:T(8,128)(2,1)} custom-call(bf16[4096,1024]{1,0:T(8,128)(2,1)S(1)} %get-tuple-element.45.refs_2_.refs_0_, bf16[4096,1024]{1,0:T(8,128)(2,1)S(1)} %get-tuple-element.52.refs_1_, bf16[16,64,256]{2,1,0:T(8,128)(2,1)S(1)} %all-to-all-done.refs_1_.refs_2_, bf16[8,64,256]{2,1,0:T(8,128)(2,1)S(1)} %collective-permute-done.7.refs_3_, ...), custom_call_target="tpu_custom_call" | custom-call | bytes 18612224 | tf_op jit(solution)/shard_map/pallas_call | solution.py:28
  39.8 3.8 %all-to-all-start.1 = ((bf16[16,128,128]{2,1,0:T(8,128)(2,1)}), bf16[16,128,128]{2,1,0:T(8,128)(2,1)S(1)}, u32[]{:S(2)}, u32[]{:S(2)}) async-start(bf16[16,128,128]{2,1,0:T(8,128)(2,1)} %shard_map.76), calls=%async_computation.1 | async-start | bytes 1048576 | tf_op jit(solution)/shard_map/all_to_all | solution.py:425
  43.6 1.9 %collective-permute-start.9 = (bf16[2,2,256,128]{3,2,1,0:T(8,128)(2,1)S(1)}, bf16[2,2,256,128]{3,2,1,0:T(8,128)(2,1)S(1)}, u32[]{:S(2)}, u32[]{:S(2)}) collective-permute-start(bf16[2,2,256,128]{3,2,1,0:T(8,128)(2,1)S(1)} %get-tuple-element.58), channel_id=1, source_target_pairs={{0,8},{2,10},{4,12},{6,14},{8,0},{10,2},{12,4},{14,6},{16,24},{18,... | collective-permute-start | bytes 786440 | tf_op jit(solution)/shard_map/ppermute | solution.py:428
  45.4 2.4 %collective-permute-start.10 = (bf16[2,2,256,128]{3,2,1,0:T(8,128)(2,1)S(1)}, bf16[2,2,256,128]{3,2,1,0:T(8,128)(2,1)S(1)}, u32[]{:S(2)}, u32[]{:S(2)}) collective-permute-start(bf16[2,2,256,128]{3,2,1,0:T(8,128)(2,1)S(1)} %get-tuple-element.59), channel_id=1, source_target_pairs={{0,24},{2,26},{4,28},{6,30},{8,16},{10,18},{12,20},{14,22},{16,8},... | collective-permute-start | bytes 786440 | tf_op jit(solution)/shard_map/ppermute | solution.py:428
  47.8 10.5 %all-to-all-done.1 = bf16[16,128,128]{2,1,0:T(8,128)(2,1)S(1)} async-done(((bf16[16,128,128]{2,1,0:T(8,128)(2,1)}), bf16[16,128,128]{2,1,0:T(8,128)(2,1)S(1)}, u32[]{:S(2)}, u32[]{:S(2)}) %all-to-all-start.1) | async-done | bytes 524320 | tf_op jit(solution)/shard_map/all_to_all | solution.py:425
  58.3 12.1 %shard_map.78 = (bf16[1,1024,128]{2,1,0:T(8,128)(2,1)S(1)}, f32[1,2048,128]{2,1,0:T(8,128)S(1)}) custom-call(bf16[1,2048,128]{2,1,0:T(8,128)(2,1)S(1)} %bitcast.28, bf16[1,2048,128]{2,1,0:T(8,128)(2,1)S(1)} %bitcast.25), custom_call_target="tpu_custom_call" | custom-call | flops 10737418240 | bytes 4194304 | tf_op jit(solution)/shard_map/pallas_call | solution.py:383
  70.4 2.3 %collective-permute-start.11 = (bf16[2,2,128,128]{3,2,1,0:T(8,128)(2,1)S(1)}, bf16[2,2,128,128]{3,2,1,0:T(8,128)(2,1)S(1)}, u32[]{:S(2)}, u32[]{:S(2)}) collective-permute-start(bf16[2,2,128,128]{3,2,1,0:T(8,128)(2,1)S(1)} %bitcast.40), channel_id=1, source_target_pairs={{0,16},{2,18},{4,20},{6,22},{8,24},{10,26},{12,28},{14,30},{16,0},... | collective-permute-start | bytes 393224 | tf_op jit(solution)/shard_map/ppermute | solution.py:428
  72.8 12.1 %shard_map.80 = (bf16[1,1024,128]{2,1,0:T(8,128)(2,1)S(1)}, bf16[1,2048,128]{2,1,0:T(8,128)(2,1)S(1)}, bf16[4096,1024]{1,0:T(8,128)(2,1)S(1)}, bf16[4096,1024]{1,0:T(8,128)(2,1)S(1)}) custom-call(bf16[1,2048,128]{2,1,0:T(8,128)(2,1)S(1)} %bitcast.29, bf16[1,2048,128]{2,1,0:T(8,128)(2,1)S(1)} %bitcast.26, ...), custom_call_target="tpu_custom_call" | custom-call | flops 10737418240 | bytes 4194304 | tf_op jit(solution)/shard_map/pallas_call | solution.py:383
  84.9 17.6 %all_to_all.20.refs_0_ = bf16[16,128,128]{2,1,0:T(8,128)(2,1)S(1)} all-to-all(bf16[16,128,128]{2,1,0:T(8,128)(2,1)S(1)} %bitcast.27), channel_id=1, replica_groups={{0,2,4,6,8,10,12,14,16,18,20,22,24,26,28,30},{1,3,5,7,9,11,13,15,17,19,..., dimensions={0} | all-to-all | bytes 1048576 | tf_op jit(solution)/shard_map/all_to_all | solution.py:425
  102.5 2.5 %shard_map.81.refs_1_ = bf16[8,64,256]{2,1,0:T(8,128)(2,1)S(1)} custom-call(bf16[16,128,128]{2,1,0:T(8,128)(2,1)S(1)} %all_to_all.20.refs_0_, bf16[4096,1024]{1,0:T(8,128)(2,1)S(1)} %get-tuple-element.64.refs_1_, bf16[4096,1024]{1,0:T(8,128)(2,1)S(1)} %get-tuple-element.65.refs_2_), custom_call_target="tpu_custom_call" | custom-call | flops 536870912 | bytes 17301504 | tf_op jit(solution)/shard_map/pallas_call | solution.py:28
  105.0 1.6 %collective-permute-start.14 = (bf16[8,64,256]{2,1,0:T(8,128)(2,1)S(1)}, bf16[8,64,256]{2,1,0:T(8,128)(2,1)S(1)}, u32[]{:S(2)}, u32[]{:S(2)}) collective-permute-start(bf16[8,64,256]{2,1,0:T(8,128)(2,1)S(1)} %shard_map.81.refs_1_), channel_id=1, source_target_pairs={{0,1},{1,0},{2,3},{3,2},{4,5},{5,4},{6,7},{7,6},{8,9},{9,8},{10,11... | collective-permute-start | bytes 786440 | tf_op jit(solution)/shard_map/ppermute | solution.py:442
  106.5 2.5 %shard_map.82.refs_2_ = bf16[8,64,256]{2,1,0:T(8,128)(2,1)S(1)} custom-call(bf16[16,128,128]{2,1,0:T(8,128)(2,1)S(1)} %all_to_all.20.refs_0_, bf16[4096,1024]{1,0:T(8,128)(2,1)S(1)} %get-tuple-element.64.refs_1_, bf16[4096,1024]{1,0:T(8,128)(2,1)S(1)} %get-tuple-element.65.refs_2_), custom_call_target="tpu_custom_call" | custom-call | flops 536870912 | bytes 17301504 | tf_op jit(solution)/shard_map/pallas_call | solution.py:28
  112.5 4.6 %shard_map.84.refs_0_ = f32[16,64,256]{2,1,0:T(8,128)S(1)} custom-call(bf16[16,128,128]{2,1,0:T(8,128)(2,1)S(1)} %all_to_all.20.refs_0_, bf16[4096,1024]{1,0:T(8,128)(2,1)S(1)} %get-tuple-element.64.refs_1_, bf16[4096,1024]{1,0:T(8,128)(2,1)S(1)} %get-tuple-element.65.refs_2_), custom_call_target="tpu_custom_call" | custom-call | flops 1073741824 | bytes 17301504 | tf_op jit(solution)/shard_map/pallas_call | solution.py:28
  119.9 4.2 %all-to-all-start.3 = ((bf16[16,64,256]{2,1,0:T(8,128)(2,1)}), bf16[16,64,256]{2,1,0:T(8,128)(2,1)S(1)}, u32[]{:S(2)}, u32[]{:S(2)}) async-start(bf16[16,64,256]{2,1,0:T(8,128)(2,1)} %shard_map.85.refs_4_), calls=%async_computation.3 | async-start | bytes 1048576 | tf_op jit(solution)/shard_map/all_to_all | solution.py:514
  125.9 2.0 %collective-permute-start.17 = (bf16[4,2,128,128]{3,2,1,0:T(8,128)(2,1)S(1)}, bf16[4,2,128,128]{3,2,1,0:T(8,128)(2,1)S(1)}, u32[]{:S(2)}, u32[]{:S(2)}) collective-permute-start(bf16[4,2,128,128]{3,2,1,0:T(8,128)(2,1)S(1)} %shard_map.88), channel_id=1, source_target_pairs={{0,4},{2,6},{4,0},{6,2},{8,12},{10,14},{12,8},{14,10},{16,20},{18,... | collective-permute-start | bytes 786440 | tf_op jit(solution)/shard_map/ppermute | solution.py:428
  127.8 10.0 %collective-permute-done.17.refs_2_ = bf16[4,2,128,128]{3,2,1,0:T(8,128)(2,1)S(1)} collective-permute-done((bf16[4,2,128,128]{3,2,1,0:T(8,128)(2,1)S(1)}, bf16[4,2,128,128]{3,2,1,0:T(8,128)(2,1)S(1)}, u32[]{:S(2)}, u32[]{:S(2)}) %collective-permute-start.17) | collective-permute-done | bytes 262176 | tf_op jit(solution)/shard_map/ppermute | solution.py:428
  (49 shorter events, 18.0 us)
Async XLA Ops:
  0.6 21.9 %all-to-all-start = ((bf16[16,64,256]{2,1,0:T(8,128)(2,1)}), bf16[16,64,256]{2,1,0:T(8,128)(2,1)S(1)}, u32[]{:S(2)}, u32[]{:S(2)}) async-start(bf16[16,64,256]{2,1,0:T(8,128)(2,1)} %bitcast.39), calls=%async_computation | async-start | bytes 1048576 | tf_op jit(solution)/shard_map/all_to_all | solution.py:446
  8.0 1.0 copy-start
  9.1 1.0 copy-start.1
  10.5 7.5 %collective-permute-start = (bf16[1,2,256,128]{3,2,1,0:T(8,128)(2,1)S(1)}, bf16[1,2,256,128]{3,2,1,0:T(8,128)(2,1)S(1)}, u32[]{:S(2)}, u32[]{:S(2)}) collective-permute-start(bf16[1,2,256,128]{3,2,1,0:T(8,128)(2,1)S(1)} %get-tuple-element.41), channel_id=1, source_target_pairs={{0,4},{2,6},{4,0},{6,2},{8,12},{10,14},{12,8},{14,10},{16,20},{18,... | collective-permute-start | bytes 393224 | tf_op jit(solution)/shard_map/ppermute | solution.py:428
  18.0 1.4 %collective-permute-start.1 = (bf16[2,256,128]{2,1,0:T(8,128)(2,1)S(1)}, bf16[2,256,128]{2,1,0:T(8,128)(2,1)S(1)}, u32[]{:S(2)}, u32[]{:S(2)}) collective-permute-start(bf16[2,256,128]{2,1,0:T(8,128)(2,1)S(1)} %get-tuple-element.43), channel_id=1, source_target_pairs={{0,2},{2,0},{4,6},{6,4},{8,10},{10,8},{12,14},{14,12},{16,18},{18,... | collective-permute-start | bytes 393224 | tf_op jit(solution)/shard_map/ppermute | solution.py:428
  22.5 11.1 %collective-permute-start.2 = (bf16[3,2,256,128]{3,2,1,0:T(8,128)(2,1)S(1)}, bf16[3,2,256,128]{3,2,1,0:T(8,128)(2,1)S(1)}, u32[]{:S(2)}, u32[]{:S(2)}) collective-permute-start(bf16[3,2,256,128]{3,2,1,0:T(8,128)(2,1)S(1)} %shard_map.71), channel_id=1, source_target_pairs={{0,4},{2,6},{4,0},{6,2},{8,12},{10,14},{12,8},{14,10},{16,20},{18,... | collective-permute-start | bytes 1179656 | tf_op jit(solution)/shard_map/ppermute | solution.py:428
  23.0 11.2 %collective-permute-start.8 = (bf16[8,64,256]{2,1,0:T(8,128)(2,1)S(1)}, bf16[8,64,256]{2,1,0:T(8,128)(2,1)S(1)}, u32[]{:S(2)}, u32[]{:S(2)}) collective-permute-start(bf16[8,64,256]{2,1,0:T(8,128)(2,1)S(1)} %get-tuple-element.74), channel_id=1, source_target_pairs={{0,1},{1,0},{2,3},{3,2},{4,5},{5,4},{6,7},{7,6},{8,9},{9,8},{10,11... | collective-permute-start | bytes 786440 | tf_op jit(solution)/shard_map/ppermute | solution.py:442
  24.6 12.8 %collective-permute-start.7 = (bf16[8,64,256]{2,1,0:T(8,128)(2,1)S(1)}, bf16[8,64,256]{2,1,0:T(8,128)(2,1)S(1)}, u32[]{:S(2)}, u32[]{:S(2)}) collective-permute-start(bf16[8,64,256]{2,1,0:T(8,128)(2,1)S(1)} %get-tuple-element.75), channel_id=1, source_target_pairs={{0,1},{1,0},{2,3},{3,2},{4,5},{5,4},{6,7},{7,6},{8,9},{9,8},{10,11... | collective-permute-start | bytes 786440 | tf_op jit(solution)/shard_map/ppermute | solution.py:442
  25.1 14.7 %collective-permute-start.6 = (bf16[2,2,256,128]{3,2,1,0:T(8,128)(2,1)S(1)}, bf16[2,2,256,128]{3,2,1,0:T(8,128)(2,1)S(1)}, u32[]{:S(2)}, u32[]{:S(2)}) collective-permute-start(bf16[2,2,256,128]{3,2,1,0:T(8,128)(2,1)S(1)} %shard_map.70), channel_id=1, source_target_pairs={{0,16},{2,18},{4,20},{6,22},{8,24},{10,26},{12,28},{14,30},{16,0},... | collective-permute-start | bytes 786440 | tf_op jit(solution)/shard_map/ppermute | solution.py:428
  33.7 2.0 %collective-permute-start.3 = (bf16[2,256,128]{2,1,0:T(8,128)(2,1)S(1)}, bf16[2,256,128]{2,1,0:T(8,128)(2,1)S(1)}, u32[]{:S(2)}, u32[]{:S(2)}) collective-permute-start(bf16[2,256,128]{2,1,0:T(8,128)(2,1)S(1)} %get-tuple-element.47), channel_id=1, source_target_pairs={{0,2},{2,0},{4,6},{6,4},{8,10},{10,8},{12,14},{14,12},{16,18},{18,... | collective-permute-start | bytes 393224 | tf_op jit(solution)/shard_map/ppermute | solution.py:428
  33.8 1.9 %collective-permute-start.4 = (bf16[2,256,128]{2,1,0:T(8,128)(2,1)S(1)}, bf16[2,256,128]{2,1,0:T(8,128)(2,1)S(1)}, u32[]{:S(2)}, u32[]{:S(2)}) collective-permute-start(bf16[2,256,128]{2,1,0:T(8,128)(2,1)S(1)} %get-tuple-element.48), channel_id=1, source_target_pairs={{0,2},{2,0},{4,6},{6,4},{8,10},{10,8},{12,14},{14,12},{16,18},{18,... | collective-permute-start | bytes 393224 | tf_op jit(solution)/shard_map/ppermute | solution.py:428
  34.3 1.4 %collective-permute-start.5 = (bf16[2,256,128]{2,1,0:T(8,128)(2,1)S(1)}, bf16[2,256,128]{2,1,0:T(8,128)(2,1)S(1)}, u32[]{:S(2)}, u32[]{:S(2)}) collective-permute-start(bf16[2,256,128]{2,1,0:T(8,128)(2,1)S(1)} %get-tuple-element.49), channel_id=1, source_target_pairs={{0,2},{2,0},{4,6},{6,4},{8,10},{10,8},{12,14},{14,12},{16,18},{18,... | collective-permute-start | bytes 393224 | tf_op jit(solution)/shard_map/ppermute | solution.py:428
  39.8 18.5 %all-to-all-start.1 = ((bf16[16,128,128]{2,1,0:T(8,128)(2,1)}), bf16[16,128,128]{2,1,0:T(8,128)(2,1)S(1)}, u32[]{:S(2)}, u32[]{:S(2)}) async-start(bf16[16,128,128]{2,1,0:T(8,128)(2,1)} %shard_map.76), calls=%async_computation.1 | async-start | bytes 1048576 | tf_op jit(solution)/shard_map/all_to_all | solution.py:425
  43.6 29.2 %collective-permute-start.9 = (bf16[2,2,256,128]{3,2,1,0:T(8,128)(2,1)S(1)}, bf16[2,2,256,128]{3,2,1,0:T(8,128)(2,1)S(1)}, u32[]{:S(2)}, u32[]{:S(2)}) collective-permute-start(bf16[2,2,256,128]{3,2,1,0:T(8,128)(2,1)S(1)} %get-tuple-element.58), channel_id=1, source_target_pairs={{0,8},{2,10},{4,12},{6,14},{8,0},{10,2},{12,4},{14,6},{16,24},{18,... | collective-permute-start | bytes 786440 | tf_op jit(solution)/shard_map/ppermute | solution.py:428
  45.4 27.3 %collective-permute-start.10 = (bf16[2,2,256,128]{3,2,1,0:T(8,128)(2,1)S(1)}, bf16[2,2,256,128]{3,2,1,0:T(8,128)(2,1)S(1)}, u32[]{:S(2)}, u32[]{:S(2)}) collective-permute-start(bf16[2,2,256,128]{3,2,1,0:T(8,128)(2,1)S(1)} %get-tuple-element.59), channel_id=1, source_target_pairs={{0,24},{2,26},{4,28},{6,30},{8,16},{10,18},{12,20},{14,22},{16,8},... | collective-permute-start | bytes 786440 | tf_op jit(solution)/shard_map/ppermute | solution.py:428
  70.4 14.5 %collective-permute-start.11 = (bf16[2,2,128,128]{3,2,1,0:T(8,128)(2,1)S(1)}, bf16[2,2,128,128]{3,2,1,0:T(8,128)(2,1)S(1)}, u32[]{:S(2)}, u32[]{:S(2)}) collective-permute-start(bf16[2,2,128,128]{3,2,1,0:T(8,128)(2,1)S(1)} %bitcast.40), channel_id=1, source_target_pairs={{0,16},{2,18},{4,20},{6,22},{8,24},{10,26},{12,28},{14,30},{16,0},... | collective-permute-start | bytes 393224 | tf_op jit(solution)/shard_map/ppermute | solution.py:428
  105.0 14.1 %collective-permute-start.14 = (bf16[8,64,256]{2,1,0:T(8,128)(2,1)S(1)}, bf16[8,64,256]{2,1,0:T(8,128)(2,1)S(1)}, u32[]{:S(2)}, u32[]{:S(2)}) collective-permute-start(bf16[8,64,256]{2,1,0:T(8,128)(2,1)S(1)} %shard_map.81.refs_1_), channel_id=1, source_target_pairs={{0,1},{1,0},{2,3},{3,2},{4,5},{5,4},{6,7},{7,6},{8,9},{9,8},{10,11... | collective-permute-start | bytes 786440 | tf_op jit(solution)/shard_map/ppermute | solution.py:442
  109.0 10.0 %collective-permute-start.15 = (bf16[8,64,256]{2,1,0:T(8,128)(2,1)S(1)}, bf16[8,64,256]{2,1,0:T(8,128)(2,1)S(1)}, u32[]{:S(2)}, u32[]{:S(2)}) collective-permute-start(bf16[8,64,256]{2,1,0:T(8,128)(2,1)S(1)} %shard_map.82.refs_2_), channel_id=1, source_target_pairs={{0,1},{1,0},{2,3},{3,2},{4,5},{5,4},{6,7},{7,6},{8,9},{9,8},{10,11... | collective-permute-start | bytes 786440 | tf_op jit(solution)/shard_map/ppermute | solution.py:442
  109.6 8.2 %collective-permute-start.13 = (bf16[2,2,128,128]{3,2,1,0:T(8,128)(2,1)S(1)}, bf16[2,2,128,128]{3,2,1,0:T(8,128)(2,1)S(1)}, u32[]{:S(2)}, u32[]{:S(2)}) collective-permute-start(bf16[2,2,128,128]{3,2,1,0:T(8,128)(2,1)S(1)} %get-tuple-element.76), channel_id=1, source_target_pairs={{0,24},{2,26},{4,28},{6,30},{8,16},{10,18},{12,20},{14,22},{16,8},... | collective-permute-start | bytes 393224 | tf_op jit(solution)/shard_map/ppermute | solution.py:428
  111.1 8.0 %collective-permute-start.12 = (bf16[2,2,128,128]{3,2,1,0:T(8,128)(2,1)S(1)}, bf16[2,2,128,128]{3,2,1,0:T(8,128)(2,1)S(1)}, u32[]{:S(2)}, u32[]{:S(2)}) collective-permute-start(bf16[2,2,128,128]{3,2,1,0:T(8,128)(2,1)S(1)} %get-tuple-element.77), channel_id=1, source_target_pairs={{0,8},{2,10},{4,12},{6,14},{8,0},{10,2},{12,4},{14,6},{16,24},{18,... | collective-permute-start | bytes 393224 | tf_op jit(solution)/shard_map/ppermute | solution.py:428
  119.9 19.0 %all-to-all-start.3 = ((bf16[16,64,256]{2,1,0:T(8,128)(2,1)}), bf16[16,64,256]{2,1,0:T(8,128)(2,1)S(1)}, u32[]{:S(2)}, u32[]{:S(2)}) async-start(bf16[16,64,256]{2,1,0:T(8,128)(2,1)} %shard_map.85.refs_4_), calls=%async_computation.3 | async-start | bytes 1048576 | tf_op jit(solution)/shard_map/all_to_all | solution.py:514
  124.2 1.6 %collective-permute-start.16 = (bf16[4,2,128,128]{3,2,1,0:T(8,128)(2,1)S(1)}, bf16[4,2,128,128]{3,2,1,0:T(8,128)(2,1)S(1)}, u32[]{:S(2)}, u32[]{:S(2)}) collective-permute-start(bf16[4,2,128,128]{3,2,1,0:T(8,128)(2,1)S(1)} %get-tuple-element.68), channel_id=1, source_target_pairs={{0,2},{2,0},{4,6},{6,4},{8,10},{10,8},{12,14},{14,12},{16,18},{18,... | collective-permute-start | bytes 786440 | tf_op jit(solution)/shard_map/ppermute | solution.py:428
  125.9 12.0 %collective-permute-start.17 = (bf16[4,2,128,128]{3,2,1,0:T(8,128)(2,1)S(1)}, bf16[4,2,128,128]{3,2,1,0:T(8,128)(2,1)S(1)}, u32[]{:S(2)}, u32[]{:S(2)}) collective-permute-start(bf16[4,2,128,128]{3,2,1,0:T(8,128)(2,1)S(1)} %shard_map.88), channel_id=1, source_target_pairs={{0,4},{2,6},{4,0},{6,2},{8,12},{10,14},{12,8},{14,10},{16,20},{18,... | collective-permute-start | bytes 786440 | tf_op jit(solution)/shard_map/ppermute | solution.py:428

commit v4 on v3

--- a/solution.py
+++ b/solution.py
@@ -370,7 +370,7 @@
             fetch.wait()
 
 
-def attention(qg, kv, rows, before=None, weights=(), block=2048, tile=256, chunk=512):
+def attention(qg, kv, rows, before=None, weights=(), block=2048, tile=512, chunk=512):
     heads, tgt, wide = qg.shape
     src = kv.shape[1]
     first, last = before is None, bool(weights)

time: 140 us -> 140 us (level)
  no operation moved by 1% of the time
where the time goes in v4:
time: 140 us; the launch traced here: 139 us
  Pallas kernels  45.3 us (32%)
  starting transfers between devices  36.5 us (26%)
  waiting for transfers between devices  36.1 us (26%)
  blocking collectives  17.6 us (13%)
  local copies, waits for them, and re-layouts  2.95 us (2%)
    pallas_call x2, Pallas kernels, attention(): pl.pallas_call(functools.partial(attention_kernel, tile, math.gcd(src, ch...  23.8 us
    ppermute x14, waiting for transfers between devices, swap(): return lax.ppermute(x, 'seq', [(i, i ^ bits) for i in range(seq)])  20.9 us
    all_to_all x1, blocking collectives, deal(): lax.all_to_all(x, 'seq', 0, 0, tiled=True, axis_index_groups=same_range)  17.6 us
    ppermute x14, starting transfers between devices, swap(): return lax.ppermute(x, 'seq', [(i, i ^ bits) for i in range(seq)])  16.9 us
    pallas_call x19, Pallas kernels, whole(): pl.pallas_call(lambda *refs: kernel(*refs[:n], *refs[n + len(after):]), i...  15.7 us
    all_to_all x1, waiting for transfers between devices, deal(): lax.all_to_all(x, 'seq', 0, 0, tiled=True, axis_index_groups=same_range)  10.5 us
    all_to_all x1, starting transfers between devices, local(): own = lax.all_to_all(memory.reshape(seq, rows, -1), 'seq', 0, 0, tiled=True)  7.4 us
    pallas_call x1, Pallas kernels, fetch(): pl.pallas_call(kernel, in_specs=[anywhere] * (n + len(after)), out_specs=...  5.78 us
  transfers between devices with their start and end apart: 21, of which 11 were waited for; matrix products, arithmetic and copies ran while one was open for 0% of the time, Pallas kernels for 30%

profile of v4, /device:TPU:0, one launch (start us, length us, event | category | flops | bytes accessed | tf_op | source)
XLA Modules:
  0.0 139.3 jit_solution(7734439750567695712)
XLA Ops:
  0.6 7.4 %all-to-all-start = ((bf16[16,64,256]{2,1,0:T(8,128)(2,1)}), bf16[16,64,256]{2,1,0:T(8,128)(2,1)S(1)}, u32[]{:S(2)}, u32[]{:S(2)}) async-start(bf16[16,64,256]{2,1,0:T(8,128)(2,1)} %bitcast.39), calls=%async_computation | async-start | bytes 1048576 | tf_op jit(solution)/shard_map/all_to_all | solution.py:446
  10.5 2.0 %collective-permute-start = (bf16[1,2,256,128]{3,2,1,0:T(8,128)(2,1)S(1)}, bf16[1,2,256,128]{3,2,1,0:T(8,128)(2,1)S(1)}, u32[]{:S(2)}, u32[]{:S(2)}) collective-permute-start(bf16[1,2,256,128]{3,2,1,0:T(8,128)(2,1)S(1)} %get-tuple-element.41), channel_id=1, source_target_pairs={{0,4},{2,6},{4,0},{6,2},{8,12},{10,14},{12,8},{14,10},{16,20},{18,... | collective-permute-start | bytes 393224 | tf_op jit(solution)/shard_map/ppermute | solution.py:428
  12.5 5.5 %collective-permute-done.refs_1_ = bf16[1,2,256,128]{3,2,1,0:T(8,128)(2,1)S(1)} collective-permute-done((bf16[1,2,256,128]{3,2,1,0:T(8,128)(2,1)S(1)}, bf16[1,2,256,128]{3,2,1,0:T(8,128)(2,1)S(1)}, u32[]{:S(2)}, u32[]{:S(2)}) %collective-permute-start) | collective-permute-done | bytes 131104 | tf_op jit(solution)/shard_map/ppermute | solution.py:428
  19.5 3.0 %all-to-all-done.refs_1_.refs_2_ = bf16[16,64,256]{2,1,0:T(8,128)(2,1)S(1)} async-done(((bf16[16,64,256]{2,1,0:T(8,128)(2,1)}), bf16[16,64,256]{2,1,0:T(8,128)(2,1)S(1)}, u32[]{:S(2)}, u32[]{:S(2)}) %all-to-all-start) | async-done | bytes 524320 | tf_op jit(solution)/shard_map/all_to_all | solution.py:446
  23.0 1.6 %collective-permute-start.8 = (bf16[8,64,256]{2,1,0:T(8,128)(2,1)S(1)}, bf16[8,64,256]{2,1,0:T(8,128)(2,1)S(1)}, u32[]{:S(2)}, u32[]{:S(2)}) collective-permute-start(bf16[8,64,256]{2,1,0:T(8,128)(2,1)S(1)} %get-tuple-element.74), channel_id=1, source_target_pairs={{0,1},{1,0},{2,3},{3,2},{4,5},{5,4},{6,7},{7,6},{8,9},{9,8},{10,11... | collective-permute-start | bytes 786440 | tf_op jit(solution)/shard_map/ppermute | solution.py:442
  25.1 1.9 %collective-permute-start.6 = (bf16[2,2,256,128]{3,2,1,0:T(8,128)(2,1)S(1)}, bf16[2,2,256,128]{3,2,1,0:T(8,128)(2,1)S(1)}, u32[]{:S(2)}, u32[]{:S(2)}) collective-permute-start(bf16[2,2,256,128]{3,2,1,0:T(8,128)(2,1)S(1)} %shard_map.70), channel_id=1, source_target_pairs={{0,16},{2,18},{4,20},{6,22},{8,24},{10,26},{12,28},{14,30},{16,0},... | collective-permute-start | bytes 786440 | tf_op jit(solution)/shard_map/ppermute | solution.py:428
  27.0 5.8 %shard_map.72 = (bf16[4096,1024]{1,0:T(8,128)(2,1)S(1)}, bf16[4096,1024]{1,0:T(8,128)(2,1)S(1)}) custom-call(bf16[4096,1024]{1,0:T(8,128)(2,1)} %refs_1_.5, bf16[4096,1024]{1,0:T(8,128)(2,1)} %refs_2_.3, bf16[16,64,256]{2,1,0:T(8,128)(2,1)S(1)} %all-to-all-done.refs_1_.refs_2_), custom_call_target="tpu_custom_call" | custom-call | bytes 16777216 | tf_op jit(solution)/shard_map/pallas_call | solution.py:137
  35.7 1.7 %collective-permute-done.7.refs_3_ = bf16[8,64,256]{2,1,0:T(8,128)(2,1)S(1)} collective-permute-done((bf16[8,64,256]{2,1,0:T(8,128)(2,1)S(1)}, bf16[8,64,256]{2,1,0:T(8,128)(2,1)S(1)}, u32[]{:S(2)}, u32[]{:S(2)}) %collective-permute-start.7) | collective-permute-done | bytes 262176 | tf_op jit(solution)/shard_map/ppermute | solution.py:442
  37.4 2.2 %shard_map.76 = bf16[16,128,128]{2,1,0:T(8,128)(2,1)} custom-call(bf16[4096,1024]{1,0:T(8,128)(2,1)S(1)} %get-tuple-element.45.refs_2_.refs_0_, bf16[4096,1024]{1,0:T(8,128)(2,1)S(1)} %get-tuple-element.52.refs_1_, bf16[16,64,256]{2,1,0:T(8,128)(2,1)S(1)} %all-to-all-done.refs_1_.refs_2_, bf16[8,64,256]{2,1,0:T(8,128)(2,1)S(1)} %collective-permute-done.7.refs_3_, ...), custom_call_target="tpu_custom_call" | custom-call | bytes 18612224 | tf_op jit(solution)/shard_map/pallas_call | solution.py:28
  39.8 3.8 %all-to-all-start.1 = ((bf16[16,128,128]{2,1,0:T(8,128)(2,1)}), bf16[16,128,128]{2,1,0:T(8,128)(2,1)S(1)}, u32[]{:S(2)}, u32[]{:S(2)}) async-start(bf16[16,128,128]{2,1,0:T(8,128)(2,1)} %shard_map.76), calls=%async_computation.1 | async-start | bytes 1048576 | tf_op jit(solution)/shard_map/all_to_all | solution.py:425
  43.6 1.9 %collective-permute-start.9 = (bf16[2,2,256,128]{3,2,1,0:T(8,128)(2,1)S(1)}, bf16[2,2,256,128]{3,2,1,0:T(8,128)(2,1)S(1)}, u32[]{:S(2)}, u32[]{:S(2)}) collective-permute-start(bf16[2,2,256,128]{3,2,1,0:T(8,128)(2,1)S(1)} %get-tuple-element.58), channel_id=1, source_target_pairs={{0,8},{2,10},{4,12},{6,14},{8,0},{10,2},{12,4},{14,6},{16,24},{18,... | collective-permute-start | bytes 786440 | tf_op jit(solution)/shard_map/ppermute | solution.py:428
  45.4 2.4 %collective-permute-start.10 = (bf16[2,2,256,128]{3,2,1,0:T(8,128)(2,1)S(1)}, bf16[2,2,256,128]{3,2,1,0:T(8,128)(2,1)S(1)}, u32[]{:S(2)}, u32[]{:S(2)}) collective-permute-start(bf16[2,2,256,128]{3,2,1,0:T(8,128)(2,1)S(1)} %get-tuple-element.59), channel_id=1, source_target_pairs={{0,24},{2,26},{4,28},{6,30},{8,16},{10,18},{12,20},{14,22},{16,8},... | collective-permute-start | bytes 786440 | tf_op jit(solution)/shard_map/ppermute | solution.py:428
  47.8 10.5 %all-to-all-done.1 = bf16[16,128,128]{2,1,0:T(8,128)(2,1)S(1)} async-done(((bf16[16,128,128]{2,1,0:T(8,128)(2,1)}), bf16[16,128,128]{2,1,0:T(8,128)(2,1)S(1)}, u32[]{:S(2)}, u32[]{:S(2)}) %all-to-all-start.1) | async-done | bytes 524320 | tf_op jit(solution)/shard_map/all_to_all | solution.py:425
  58.3 11.8 %shard_map.78 = (bf16[1,1024,128]{2,1,0:T(8,128)(2,1)S(1)}, f32[1,2048,128]{2,1,0:T(8,128)S(1)}) custom-call(bf16[1,2048,128]{2,1,0:T(8,128)(2,1)S(1)} %bitcast.28, bf16[1,2048,128]{2,1,0:T(8,128)(2,1)S(1)} %bitcast.25), custom_call_target="tpu_custom_call" | custom-call | flops 10737418240 | bytes 4194304 | tf_op jit(solution)/shard_map/pallas_call | solution.py:383
  70.1 2.3 %collective-permute-start.11 = (bf16[2,2,128,128]{3,2,1,0:T(8,128)(2,1)S(1)}, bf16[2,2,128,128]{3,2,1,0:T(8,128)(2,1)S(1)}, u32[]{:S(2)}, u32[]{:S(2)}) collective-permute-start(bf16[2,2,128,128]{3,2,1,0:T(8,128)(2,1)S(1)} %bitcast.40), channel_id=1, source_target_pairs={{0,16},{2,18},{4,20},{6,22},{8,24},{10,26},{12,28},{14,30},{16,0},... | collective-permute-start | bytes 393224 | tf_op jit(solution)/shard_map/ppermute | solution.py:428
  72.5 12.0 %shard_map.80 = (bf16[1,1024,128]{2,1,0:T(8,128)(2,1)S(1)}, bf16[1,2048,128]{2,1,0:T(8,128)(2,1)S(1)}, bf16[4096,1024]{1,0:T(8,128)(2,1)S(1)}, bf16[4096,1024]{1,0:T(8,128)(2,1)S(1)}) custom-call(bf16[1,2048,128]{2,1,0:T(8,128)(2,1)S(1)} %bitcast.29, bf16[1,2048,128]{2,1,0:T(8,128)(2,1)S(1)} %bitcast.26, ...), custom_call_target="tpu_custom_call" | custom-call | flops 10737418240 | bytes 4194304 | tf_op jit(solution)/shard_map/pallas_call | solution.py:383
  84.5 17.6 %all_to_all.20.refs_0_ = bf16[16,128,128]{2,1,0:T(8,128)(2,1)S(1)} all-to-all(bf16[16,128,128]{2,1,0:T(8,128)(2,1)S(1)} %bitcast.27), channel_id=1, replica_groups={{0,2,4,6,8,10,12,14,16,18,20,22,24,26,28,30},{1,3,5,7,9,11,13,15,17,19,..., dimensions={0} | all-to-all | bytes 1048576 | tf_op jit(solution)/shard_map/all_to_all | solution.py:425
  102.1 2.5 %shard_map.81.refs_1_ = bf16[8,64,256]{2,1,0:T(8,128)(2,1)S(1)} custom-call(bf16[16,128,128]{2,1,0:T(8,128)(2,1)S(1)} %all_to_all.20.refs_0_, bf16[4096,1024]{1,0:T(8,128)(2,1)S(1)} %get-tuple-element.64.refs_1_, bf16[4096,1024]{1,0:T(8,128)(2,1)S(1)} %get-tuple-element.65.refs_2_), custom_call_target="tpu_custom_call" | custom-call | flops 536870912 | bytes 17301504 | tf_op jit(solution)/shard_map/pallas_call | solution.py:28
  104.5 1.6 %collective-permute-start.14 = (bf16[8,64,256]{2,1,0:T(8,128)(2,1)S(1)}, bf16[8,64,256]{2,1,0:T(8,128)(2,1)S(1)}, u32[]{:S(2)}, u32[]{:S(2)}) collective-permute-start(bf16[8,64,256]{2,1,0:T(8,128)(2,1)S(1)} %shard_map.81.refs_1_), channel_id=1, source_target_pairs={{0,1},{1,0},{2,3},{3,2},{4,5},{5,4},{6,7},{7,6},{8,9},{9,8},{10,11... | collective-permute-start | bytes 786440 | tf_op jit(solution)/shard_map/ppermute | solution.py:442
  106.1 2.5 %shard_map.82.refs_2_ = bf16[8,64,256]{2,1,0:T(8,128)(2,1)S(1)} custom-call(bf16[16,128,128]{2,1,0:T(8,128)(2,1)S(1)} %all_to_all.20.refs_0_, bf16[4096,1024]{1,0:T(8,128)(2,1)S(1)} %get-tuple-element.64.refs_1_, bf16[4096,1024]{1,0:T(8,128)(2,1)S(1)} %get-tuple-element.65.refs_2_), custom_call_target="tpu_custom_call" | custom-call | flops 536870912 | bytes 17301504 | tf_op jit(solution)/shard_map/pallas_call | solution.py:28
  112.1 4.6 %shard_map.84.refs_0_ = f32[16,64,256]{2,1,0:T(8,128)S(1)} custom-call(bf16[16,128,128]{2,1,0:T(8,128)(2,1)S(1)} %all_to_all.20.refs_0_, bf16[4096,1024]{1,0:T(8,128)(2,1)S(1)} %get-tuple-element.64.refs_1_, bf16[4096,1024]{1,0:T(8,128)(2,1)S(1)} %get-tuple-element.65.refs_2_), custom_call_target="tpu_custom_call" | custom-call | flops 1073741824 | bytes 17301504 | tf_op jit(solution)/shard_map/pallas_call | solution.py:28
  119.5 4.2 %all-to-all-start.3 = ((bf16[16,64,256]{2,1,0:T(8,128)(2,1)}), bf16[16,64,256]{2,1,0:T(8,128)(2,1)S(1)}, u32[]{:S(2)}, u32[]{:S(2)}) async-start(bf16[16,64,256]{2,1,0:T(8,128)(2,1)} %shard_map.85.refs_4_), calls=%async_computation.3 | async-start | bytes 1048576 | tf_op jit(solution)/shard_map/all_to_all | solution.py:514
  125.4 2.0 %collective-permute-start.17 = (bf16[4,2,128,128]{3,2,1,0:T(8,128)(2,1)S(1)}, bf16[4,2,128,128]{3,2,1,0:T(8,128)(2,1)S(1)}, u32[]{:S(2)}, u32[]{:S(2)}) collective-permute-start(bf16[4,2,128,128]{3,2,1,0:T(8,128)(2,1)S(1)} %shard_map.88), channel_id=1, source_target_pairs={{0,4},{2,6},{4,0},{6,2},{8,12},{10,14},{12,8},{14,10},{16,20},{18,... | collective-permute-start | bytes 786440 | tf_op jit(solution)/shard_map/ppermute | solution.py:428
  127.4 10.0 %collective-permute-done.17.refs_2_ = bf16[4,2,128,128]{3,2,1,0:T(8,128)(2,1)S(1)} collective-permute-done((bf16[4,2,128,128]{3,2,1,0:T(8,128)(2,1)S(1)}, bf16[4,2,128,128]{3,2,1,0:T(8,128)(2,1)S(1)}, u32[]{:S(2)}, u32[]{:S(2)}) %collective-permute-start.17) | collective-permute-done | bytes 262176 | tf_op jit(solution)/shard_map/ppermute | solution.py:428
  (49 shorter events, 18.0 us)
Async XLA Ops:
  0.6 21.9 %all-to-all-start = ((bf16[16,64,256]{2,1,0:T(8,128)(2,1)}), bf16[16,64,256]{2,1,0:T(8,128)(2,1)S(1)}, u32[]{:S(2)}, u32[]{:S(2)}) async-start(bf16[16,64,256]{2,1,0:T(8,128)(2,1)} %bitcast.39), calls=%async_computation | async-start | bytes 1048576 | tf_op jit(solution)/shard_map/all_to_all | solution.py:446
  8.0 1.0 copy-start
  9.1 1.0 copy-start.1
  10.5 7.5 %collective-permute-start = (bf16[1,2,256,128]{3,2,1,0:T(8,128)(2,1)S(1)}, bf16[1,2,256,128]{3,2,1,0:T(8,128)(2,1)S(1)}, u32[]{:S(2)}, u32[]{:S(2)}) collective-permute-start(bf16[1,2,256,128]{3,2,1,0:T(8,128)(2,1)S(1)} %get-tuple-element.41), channel_id=1, source_target_pairs={{0,4},{2,6},{4,0},{6,2},{8,12},{10,14},{12,8},{14,10},{16,20},{18,... | collective-permute-start | bytes 393224 | tf_op jit(solution)/shard_map/ppermute | solution.py:428
  18.0 1.4 %collective-permute-start.1 = (bf16[2,256,128]{2,1,0:T(8,128)(2,1)S(1)}, bf16[2,256,128]{2,1,0:T(8,128)(2,1)S(1)}, u32[]{:S(2)}, u32[]{:S(2)}) collective-permute-start(bf16[2,256,128]{2,1,0:T(8,128)(2,1)S(1)} %get-tuple-element.43), channel_id=1, source_target_pairs={{0,2},{2,0},{4,6},{6,4},{8,10},{10,8},{12,14},{14,12},{16,18},{18,... | collective-permute-start | bytes 393224 | tf_op jit(solution)/shard_map/ppermute | solution.py:428
  22.5 11.1 %collective-permute-start.2 = (bf16[3,2,256,128]{3,2,1,0:T(8,128)(2,1)S(1)}, bf16[3,2,256,128]{3,2,1,0:T(8,128)(2,1)S(1)}, u32[]{:S(2)}, u32[]{:S(2)}) collective-permute-start(bf16[3,2,256,128]{3,2,1,0:T(8,128)(2,1)S(1)} %shard_map.71), channel_id=1, source_target_pairs={{0,4},{2,6},{4,0},{6,2},{8,12},{10,14},{12,8},{14,10},{16,20},{18,... | collective-permute-start | bytes 1179656 | tf_op jit(solution)/shard_map/ppermute | solution.py:428
  23.0 11.2 %collective-permute-start.8 = (bf16[8,64,256]{2,1,0:T(8,128)(2,1)S(1)}, bf16[8,64,256]{2,1,0:T(8,128)(2,1)S(1)}, u32[]{:S(2)}, u32[]{:S(2)}) collective-permute-start(bf16[8,64,256]{2,1,0:T(8,128)(2,1)S(1)} %get-tuple-element.74), channel_id=1, source_target_pairs={{0,1},{1,0},{2,3},{3,2},{4,5},{5,4},{6,7},{7,6},{8,9},{9,8},{10,11... | collective-permute-start | bytes 786440 | tf_op jit(solution)/shard_map/ppermute | solution.py:442
  24.6 12.8 %collective-permute-start.7 = (bf16[8,64,256]{2,1,0:T(8,128)(2,1)S(1)}, bf16[8,64,256]{2,1,0:T(8,128)(2,1)S(1)}, u32[]{:S(2)}, u32[]{:S(2)}) collective-permute-start(bf16[8,64,256]{2,1,0:T(8,128)(2,1)S(1)} %get-tuple-element.75), channel_id=1, source_target_pairs={{0,1},{1,0},{2,3},{3,2},{4,5},{5,4},{6,7},{7,6},{8,9},{9,8},{10,11... | collective-permute-start | bytes 786440 | tf_op jit(solution)/shard_map/ppermute | solution.py:442
  25.1 14.7 %collective-permute-start.6 = (bf16[2,2,256,128]{3,2,1,0:T(8,128)(2,1)S(1)}, bf16[2,2,256,128]{3,2,1,0:T(8,128)(2,1)S(1)}, u32[]{:S(2)}, u32[]{:S(2)}) collective-permute-start(bf16[2,2,256,128]{3,2,1,0:T(8,128)(2,1)S(1)} %shard_map.70), channel_id=1, source_target_pairs={{0,16},{2,18},{4,20},{6,22},{8,24},{10,26},{12,28},{14,30},{16,0},... | collective-permute-start | bytes 786440 | tf_op jit(solution)/shard_map/ppermute | solution.py:428
  33.7 2.0 %collective-permute-start.3 = (bf16[2,256,128]{2,1,0:T(8,128)(2,1)S(1)}, bf16[2,256,128]{2,1,0:T(8,128)(2,1)S(1)}, u32[]{:S(2)}, u32[]{:S(2)}) collective-permute-start(bf16[2,256,128]{2,1,0:T(8,128)(2,1)S(1)} %get-tuple-element.47), channel_id=1, source_target_pairs={{0,2},{2,0},{4,6},{6,4},{8,10},{10,8},{12,14},{14,12},{16,18},{18,... | collective-permute-start | bytes 393224 | tf_op jit(solution)/shard_map/ppermute | solution.py:428
  33.8 1.9 %collective-permute-start.4 = (bf16[2,256,128]{2,1,0:T(8,128)(2,1)S(1)}, bf16[2,256,128]{2,1,0:T(8,128)(2,1)S(1)}, u32[]{:S(2)}, u32[]{:S(2)}) collective-permute-start(bf16[2,256,128]{2,1,0:T(8,128)(2,1)S(1)} %get-tuple-element.48), channel_id=1, source_target_pairs={{0,2},{2,0},{4,6},{6,4},{8,10},{10,8},{12,14},{14,12},{16,18},{18,... | collective-permute-start | bytes 393224 | tf_op jit(solution)/shard_map/ppermute | solution.py:428
  34.3 1.4 %collective-permute-start.5 = (bf16[2,256,128]{2,1,0:T(8,128)(2,1)S(1)}, bf16[2,256,128]{2,1,0:T(8,128)(2,1)S(1)}, u32[]{:S(2)}, u32[]{:S(2)}) collective-permute-start(bf16[2,256,128]{2,1,0:T(8,128)(2,1)S(1)} %get-tuple-element.49), channel_id=1, source_target_pairs={{0,2},{2,0},{4,6},{6,4},{8,10},{10,8},{12,14},{14,12},{16,18},{18,... | collective-permute-start | bytes 393224 | tf_op jit(solution)/shard_map/ppermute | solution.py:428
  39.8 18.5 %all-to-all-start.1 = ((bf16[16,128,128]{2,1,0:T(8,128)(2,1)}), bf16[16,128,128]{2,1,0:T(8,128)(2,1)S(1)}, u32[]{:S(2)}, u32[]{:S(2)}) async-start(bf16[16,128,128]{2,1,0:T(8,128)(2,1)} %shard_map.76), calls=%async_computation.1 | async-start | bytes 1048576 | tf_op jit(solution)/shard_map/all_to_all | solution.py:425
  43.6 28.9 %collective-permute-start.9 = (bf16[2,2,256,128]{3,2,1,0:T(8,128)(2,1)S(1)}, bf16[2,2,256,128]{3,2,1,0:T(8,128)(2,1)S(1)}, u32[]{:S(2)}, u32[]{:S(2)}) collective-permute-start(bf16[2,2,256,128]{3,2,1,0:T(8,128)(2,1)S(1)} %get-tuple-element.58), channel_id=1, source_target_pairs={{0,8},{2,10},{4,12},{6,14},{8,0},{10,2},{12,4},{14,6},{16,24},{18,... | collective-permute-start | bytes 786440 | tf_op jit(solution)/shard_map/ppermute | solution.py:428
  45.4 27.0 %collective-permute-start.10 = (bf16[2,2,256,128]{3,2,1,0:T(8,128)(2,1)S(1)}, bf16[2,2,256,128]{3,2,1,0:T(8,128)(2,1)S(1)}, u32[]{:S(2)}, u32[]{:S(2)}) collective-permute-start(bf16[2,2,256,128]{3,2,1,0:T(8,128)(2,1)S(1)} %get-tuple-element.59), channel_id=1, source_target_pairs={{0,24},{2,26},{4,28},{6,30},{8,16},{10,18},{12,20},{14,22},{16,8},... | collective-permute-start | bytes 786440 | tf_op jit(solution)/shard_map/ppermute | solution.py:428
  70.1 14.4 %collective-permute-start.11 = (bf16[2,2,128,128]{3,2,1,0:T(8,128)(2,1)S(1)}, bf16[2,2,128,128]{3,2,1,0:T(8,128)(2,1)S(1)}, u32[]{:S(2)}, u32[]{:S(2)}) collective-permute-start(bf16[2,2,128,128]{3,2,1,0:T(8,128)(2,1)S(1)} %bitcast.40), channel_id=1, source_target_pairs={{0,16},{2,18},{4,20},{6,22},{8,24},{10,26},{12,28},{14,30},{16,0},... | collective-permute-start | bytes 393224 | tf_op jit(solution)/shard_map/ppermute | solution.py:428
  104.5 14.1 %collective-permute-start.14 = (bf16[8,64,256]{2,1,0:T(8,128)(2,1)S(1)}, bf16[8,64,256]{2,1,0:T(8,128)(2,1)S(1)}, u32[]{:S(2)}, u32[]{:S(2)}) collective-permute-start(bf16[8,64,256]{2,1,0:T(8,128)(2,1)S(1)} %shard_map.81.refs_1_), channel_id=1, source_target_pairs={{0,1},{1,0},{2,3},{3,2},{4,5},{5,4},{6,7},{7,6},{8,9},{9,8},{10,11... | collective-permute-start | bytes 786440 | tf_op jit(solution)/shard_map/ppermute | solution.py:442
  108.5 10.0 %collective-permute-start.15 = (bf16[8,64,256]{2,1,0:T(8,128)(2,1)S(1)}, bf16[8,64,256]{2,1,0:T(8,128)(2,1)S(1)}, u32[]{:S(2)}, u32[]{:S(2)}) collective-permute-start(bf16[8,64,256]{2,1,0:T(8,128)(2,1)S(1)} %shard_map.82.refs_2_), channel_id=1, source_target_pairs={{0,1},{1,0},{2,3},{3,2},{4,5},{5,4},{6,7},{7,6},{8,9},{9,8},{10,11... | collective-permute-start | bytes 786440 | tf_op jit(solution)/shard_map/ppermute | solution.py:442
  109.2 8.2 %collective-permute-start.13 = (bf16[2,2,128,128]{3,2,1,0:T(8,128)(2,1)S(1)}, bf16[2,2,128,128]{3,2,1,0:T(8,128)(2,1)S(1)}, u32[]{:S(2)}, u32[]{:S(2)}) collective-permute-start(bf16[2,2,128,128]{3,2,1,0:T(8,128)(2,1)S(1)} %get-tuple-element.76), channel_id=1, source_target_pairs={{0,24},{2,26},{4,28},{6,30},{8,16},{10,18},{12,20},{14,22},{16,8},... | collective-permute-start | bytes 393224 | tf_op jit(solution)/shard_map/ppermute | solution.py:428
  110.6 8.0 %collective-permute-start.12 = (bf16[2,2,128,128]{3,2,1,0:T(8,128)(2,1)S(1)}, bf16[2,2,128,128]{3,2,1,0:T(8,128)(2,1)S(1)}, u32[]{:S(2)}, u32[]{:S(2)}) collective-permute-start(bf16[2,2,128,128]{3,2,1,0:T(8,128)(2,1)S(1)} %get-tuple-element.77), channel_id=1, source_target_pairs={{0,8},{2,10},{4,12},{6,14},{8,0},{10,2},{12,4},{14,6},{16,24},{18,... | collective-permute-start | bytes 393224 | tf_op jit(solution)/shard_map/ppermute | solution.py:428
  119.5 19.0 %all-to-all-start.3 = ((bf16[16,64,256]{2,1,0:T(8,128)(2,1)}), bf16[16,64,256]{2,1,0:T(8,128)(2,1)S(1)}, u32[]{:S(2)}, u32[]{:S(2)}) async-start(bf16[16,64,256]{2,1,0:T(8,128)(2,1)} %shard_map.85.refs_4_), calls=%async_computation.3 | async-start | bytes 1048576 | tf_op jit(solution)/shard_map/all_to_all | solution.py:514
  123.7 1.6 %collective-permute-start.16 = (bf16[4,2,128,128]{3,2,1,0:T(8,128)(2,1)S(1)}, bf16[4,2,128,128]{3,2,1,0:T(8,128)(2,1)S(1)}, u32[]{:S(2)}, u32[]{:S(2)}) collective-permute-start(bf16[4,2,128,128]{3,2,1,0:T(8,128)(2,1)S(1)} %get-tuple-element.68), channel_id=1, source_target_pairs={{0,2},{2,0},{4,6},{6,4},{8,10},{10,8},{12,14},{14,12},{16,18},{18,... | collective-permute-start | bytes 786440 | tf_op jit(solution)/shard_map/ppermute | solution.py:428
  125.4 12.0 %collective-permute-start.17 = (bf16[4,2,128,128]{3,2,1,0:T(8,128)(2,1)S(1)}, bf16[4,2,128,128]{3,2,1,0:T(8,128)(2,1)S(1)}, u32[]{:S(2)}, u32[]{:S(2)}) collective-permute-start(bf16[4,2,128,128]{3,2,1,0:T(8,128)(2,1)S(1)} %shard_map.88), channel_id=1, source_target_pairs={{0,4},{2,6},{4,0},{6,2},{8,12},{10,14},{12,8},{14,10},{16,20},{18,... | collective-permute-start | bytes 786440 | tf_op jit(solution)/shard_map/ppermute | solution.py:428
